TPU v7x, 256 devices: a whole 4x4x8 slice. The times are simulated.
256 devices in a mesh: dp: 4 (over x), mem: 64 (over z, y, core).
Axes of the slice: x: 4, y: 4, z: 8, core: 2. Of those that a mesh axis runs over, the one named last changes fastest.
Arguments:
- queries: bfloat16 [32768, 2048], P(('dp', 'mem')), may hold values from -8 to 8
- keys_local: bfloat16 [32768, 2048], P(('dp', 'mem')), may hold values from -8 to 8
- values_local: bfloat16 [32768, 2048], P(('dp', 'mem')), may hold values from -6 to 6
- mem_keys: bfloat16 [256, 16, 128, 128], P('mem'), may hold values from -8 to 8
- mem_values: bfloat16 [256, 16, 128, 128], P('mem'), may hold values from -6 to 6
- prev_keys: bfloat16 [2048, 128, 128], P(('dp', 'mem')), may hold values from -6 to 6
- prev_values: bfloat16 [2048, 128, 128], P(('dp', 'mem')), may hold values from -6 to 6
- gate_logit: float32 [16], replicated, may hold values from -2 to 2
- cotangent: bfloat16 [32768, 2048], P(('dp', 'mem')), may hold values from -4 to 4
- block_home: int32 [16, 256], replicated, may hold values from 0 to 255, as said below
- query_blocks: int32 [256, 16, 4], P(('dp', 'mem')), may hold values from 0 to 255, as said below
- write_slots: int32 [2048], P(('dp', 'mem')), may hold values from 0 to 255, as said below
Outputs:
- mixed: bfloat16 [32768, 2048], P(('dp', 'mem'))
- new_keys: bfloat16 [256, 16, 128, 128], P('mem')
- new_values: bfloat16 [256, 16, 128, 128], P('mem')
- gate_grad: float32 [16], replicated
Inputs may be any that keep to these rules, and one draw needn't show every extreme that they name: Each row block_home[h] is a permutation of the storage blocks; storage block p lies on index p // 4 of mem. `query_blocks`: of the requests of one device (its tiles, all heads), at most 2 name blocks whose storage lies on one index of mem. `write_slots`: no two units are written to the same storage block of the same head. Of the units held by the 4 devices at one index of mem, at most 1 go to storage on one index of mem.
All inputs are finite; a program needn't handle non-finite values.
Results may differ from a plain program's by a relative error of at most 0.0047.
Values may be sent and summed in bfloat16 or wider, within the bound.
A program may use at most 128 MiB of HBM per device.

v0:
```python
import math

import jax
import jax.numpy as jnp
from jax import lax
from jax.sharding import PartitionSpec as P


def attend(query_rows, key_rows, values, allowed):
    scaling = 1.0 / math.sqrt(query_rows.shape[-1])
    scores = (
        jnp.einsum("thqd,thkd->thqk", query_rows, key_rows, preferred_element_type=jnp.float32)
        * scaling
    )
    scores = jnp.where(allowed, scores, -1e30)
    shifted = jnp.exp(scores - jnp.max(scores, axis=-1, keepdims=True))
    weights = (shifted / jnp.sum(shifted, axis=-1, keepdims=True)).astype(jnp.bfloat16)
    return jnp.einsum("thqk,thkd->thqd", weights, values, preferred_element_type=jnp.float32)


def slot_rank(target):
    length = target.shape[0]
    earlier = jnp.arange(length)[:, None] > jnp.arange(length)[None, :]
    return jnp.sum((target[:, None] == target[None, :]) & earlier, axis=1)


def apply_writes(flat, codes, payload):
    beyond = flat.shape[0]
    target = jnp.where(codes >= 0, codes, beyond).reshape(-1)
    return flat.at[target].set(payload.reshape((-1,) + flat.shape[1:]), mode="drop")


def to_tiles(array, tile_dev, block_len, head_count, head_dim):
    return array.reshape(tile_dev, block_len, head_count, head_dim).transpose(0, 2, 1, 3)


def on_device(
    queries,
    keys_local,
    values_local,
    mem_keys,
    mem_values,
    prev_keys,
    prev_values,
    gate_logit,
    cotangent,
    block_home,
    query_blocks,
    write_slots,
):
    mem_size = lax.axis_size("mem")
    dp_size = lax.axis_size("dp")
    head_count = gate_logit.shape[0]
    blk_dev, _, block_len, head_dim = mem_keys.shape
    tile_dev, _, topb_count = query_blocks.shape
    units_all = blk_dev * head_count
    flat_keys = mem_keys.reshape(units_all, block_len, head_dim)
    flat_values = mem_values.reshape(units_all, block_len, head_dim)
    head_grid = jnp.broadcast_to(
        jnp.arange(head_count, dtype=jnp.int32)[None, :, None], query_blocks.shape
    )
    storage = block_home[head_grid, query_blocks].reshape(-1)
    asked_from = storage // blk_dev
    asked_code = storage % blk_dev * head_count + head_grid.reshape(-1)
    requests = asked_from.shape[0]
    capacity = max(2, 2 * requests // mem_size)
    asked_slot = asked_from * capacity + slot_rank(asked_from)
    request_box = (
        jnp.full((mem_size * capacity,), -1, jnp.int32)
        .at[asked_slot]
        .set(asked_code)
        .reshape(mem_size, capacity)
    )
    clipped = jnp.clip(
        lax.all_to_all(request_box, "mem", split_axis=0, concat_axis=0, tiled=True),
        0,
        units_all - 1,
    )
    came_keys = lax.all_to_all(flat_keys[clipped], "mem", split_axis=0, concat_axis=0, tiled=True)
    came_values = lax.all_to_all(
        flat_values[clipped], "mem", split_axis=0, concat_axis=0, tiled=True
    )
    far_keys = came_keys.reshape(mem_size * capacity, block_len, head_dim)[asked_slot].reshape(
        tile_dev, head_count, topb_count * block_len, head_dim
    )
    far_values = came_values.reshape(mem_size * capacity, block_len, head_dim)[asked_slot].reshape(
        tile_dev, head_count, topb_count * block_len, head_dim
    )
    query_tiles = to_tiles(queries, tile_dev, block_len, head_count, head_dim)
    causal = jnp.arange(block_len)[:, None] >= jnp.arange(block_len)[None, :]
    near_att = attend(
        query_tiles,
        to_tiles(keys_local, tile_dev, block_len, head_count, head_dim),
        to_tiles(values_local, tile_dev, block_len, head_count, head_dim),
        causal[None, None],
    )
    recalled = attend(query_tiles, far_keys, far_values, True)
    sigmoid_gate = jax.nn.sigmoid(gate_logit)
    opening = sigmoid_gate[None, :, None, None]
    blended = opening * recalled + (1.0 - opening) * near_att
    mixed = (
        blended.transpose(0, 2, 1, 3)
        .reshape(tile_dev * block_len, head_count * head_dim)
        .astype(jnp.bfloat16)
    )
    upstream = to_tiles(cotangent, tile_dev, block_len, head_count, head_dim).astype(jnp.float32)
    partial_value = jnp.sum(upstream * (recalled - near_att), axis=(0, 2, 3))
    grad_total = lax.psum(partial_value, ("dp", "mem"))
    gate_grad = sigmoid_gate * (1.0 - sigmoid_gate) * grad_total
    wr_dev = prev_keys.shape[0]
    inner_index = lax.axis_index("mem") * wr_dev + jnp.arange(wr_dev, dtype=jnp.int32)
    write_head = inner_index % head_count
    write_stamp = block_home[write_head, write_slots] * head_count + write_head
    write_cap = max(1, dp_size * wr_dev // mem_size)
    every_stamp = lax.all_gather(write_stamp, "dp", axis=0, tiled=True)
    every_target = every_stamp // units_all
    every_place = every_target * write_cap + slot_rank(every_target)
    own_place = lax.dynamic_slice_in_dim(every_place, lax.axis_index("dp") * wr_dev, wr_dev)
    box_shape = (mem_size * write_cap, block_len, head_dim)
    own_keys = jnp.zeros(box_shape, jnp.float32).at[own_place].set(prev_keys.astype(jnp.float32))
    own_values = (
        jnp.zeros(box_shape, jnp.float32).at[own_place].set(prev_values.astype(jnp.float32))
    )
    summed_keys, summed_values = (
        lax.psum(own_keys.astype(jnp.bfloat16), "dp").astype(jnp.float32),
        lax.psum(own_values.astype(jnp.bfloat16), "dp").astype(jnp.float32),
    )
    box_keys = summed_keys.astype(jnp.bfloat16).reshape(mem_size, write_cap, block_len, head_dim)
    box_values = summed_values.astype(jnp.bfloat16).reshape(
        mem_size, write_cap, block_len, head_dim
    )
    box_codes = (
        jnp.full((mem_size * write_cap,), -1, jnp.int32)
        .at[every_place]
        .set(every_stamp % units_all)
        .reshape(mem_size, write_cap)
    )
    got_keys, got_values, got_codes = (
        lax.all_to_all(box_keys, "mem", split_axis=0, concat_axis=0, tiled=True),
        lax.all_to_all(box_values, "mem", split_axis=0, concat_axis=0, tiled=True),
        lax.all_to_all(box_codes, "mem", split_axis=0, concat_axis=0, tiled=True),
    )
    new_keys = apply_writes(flat_keys, got_codes, got_keys).reshape(mem_keys.shape)
    new_values = apply_writes(flat_values, got_codes, got_values).reshape(mem_values.shape)
    return (mixed, new_keys, new_values, gate_grad)


def solution(mesh):
    placed = (
        P(("dp", "mem"), None),
        P(("dp", "mem"), None),
        P(("dp", "mem"), None),
        P("mem", None, None, None),
        P("mem", None, None, None),
        P(("dp", "mem"), None, None),
        P(("dp", "mem"), None, None),
        P(),
        P(("dp", "mem"), None),
        P(),
        P(("dp", "mem"), None, None),
        P(("dp", "mem")),
    )
    return jax.shard_map(
        on_device,
        mesh=mesh,
        in_specs=placed,
        out_specs=(
            P(("dp", "mem"), None),
            P("mem", None, None, None),
            P("mem", None, None, None),
            P(),
        ),
        check_vma=False,
    )
```

profile of v0, /device:TPU:1, one launch (start us, length us, event | category | flops | bytes accessed | tf_op | source)
XLA Modules:
  0.0 487.8 jit_solution(8692472882439131259)
XLA Ops:
  7.2 3.3 copy.124
  11.0 0.9 gather_fusion
  12.1 0.8 scatter_custom_fusion
  12.9 0.8 all_to_all.26
  13.7 13.2 %all-to-all-start = ((s32[64,1,2]{2,1,0:T(1,128)}), s32[64,1,2]{2,1,0:T(1,128)S(1)}, u32[]{:S(2)}, u32[]{:S(2)}) async-start(s32[64,1,2]{2,1,0:T(1,128)} %bitcast.6), calls=%async_computation | async-start | bytes 65536 | tf_op jit(solution)/shard_map/all_to_all | solution.py:75
  26.9 0.6 gather_fusion.5
  27.5 0.6 dynamic-slice
  28.9 7.4 %all-reduce = s32[32]{0:T(128)S(1)} all-reduce(s32[32]{0:T(128)S(1)} %fusion.35), channel_id=1, replica_groups=mesh['dp'=4,'mem'=64] {'dp'}, use_global_device_ids=true, to_apply=%add | all-reduce | flops 32 | bytes 256
  36.3 0.2 convert_reduce_fusion.1
  36.5 0.7 scatter_custom_fusion.1
  37.2 0.7 copy.92
  37.9 11.7 %all-to-all-start.3 = ((s32[64,1,1]{2,1,0:T(1,128)}), s32[64,1,1]{2,1,0:T(1,128)S(1)}, u32[]{:S(2)}, u32[]{:S(2)}) async-start(s32[64,1,1]{2,1,0:T(1,128)} %copy.92), calls=%async_computation.3 | async-start | bytes 65536 | tf_op jit(solution)/shard_map/all_to_all | solution.py:141
  50.0 4.6 gather_fusion.1
  54.7 4.3 all-to-all-done.3
  59.0 6.2 %all-to-all-start.1 = ((bf16[64,2,128,128]{3,2,1,0:T(8,128)(2,1)}), bf16[64,2,128,128]{3,2,1,0:T(8,128)(2,1)}, u32[]{:S(2)}, u32[]{:S(2)}) async-start(bf16[64,2,128,128]{3,2,1,0:T(8,128)(2,1)} %bitcast.129), calls=%async_computation.1 | async-start | bytes 8388608 | tf_op jit(solution)/shard_map/all_to_all | solution.py:79
  65.2 3.1 gather_fusion.3
  68.2 91.3 %all-to-all-done.1 = bf16[64,2,128,128]{3,2,1,0:T(8,128)(2,1)} async-done(((bf16[64,2,128,128]{3,2,1,0:T(8,128)(2,1)}), bf16[64,2,128,128]{3,2,1,0:T(8,128)(2,1)}, u32[]{:S(2)}, u32[]{:S(2)}) %all-to-all-start.1) | async-done | bytes 4194336 | tf_op jit(solution)/shard_map/all_to_all | solution.py:79
  159.6 7.5 %all-to-all-start.2 = ((bf16[64,2,128,128]{3,2,1,0:T(8,128)(2,1)}), bf16[64,2,128,128]{3,2,1,0:T(8,128)(2,1)}, u32[]{:S(2)}, u32[]{:S(2)}) async-start(bf16[64,2,128,128]{3,2,1,0:T(8,128)(2,1)} %bitcast.128), calls=%async_computation.2 | async-start | bytes 8388608 | tf_op jit(solution)/shard_map/all_to_all | solution.py:80
  167.3 2.4 broadcast.358.clone.1
  169.8 2.5 scatter_fusion
  172.2 2.5 broadcast.358.clone
  174.7 2.5 scatter_fusion.2
  177.2 6.5 %convert_bitcast_fusion = (bf16[64,1,128,128]{3,2,0,1:T(8,128)(2,1)}, bf16[64,1,128,128]{3,2,0,1:T(8,128)(2,1)}) fusion(f32[64,128,128]{2,1,0:T(8,128)} %scatter_fusion.2, f32[64,128,128]{2,1,0:T(8,128)} %scatter_fusion), kind=kLoop, calls=%fused_computation.20 | loop fusion | flops 2097152 | bytes 12582912 | tf_op jit(solution)/shard_map/reshape | solution.py:129
  183.7 97.4 %all-reduce.4.cloned.1.call-done = (bf16[64,1,128,128]{3,2,0,1:T(8,128)(2,1)}, bf16[64,1,128,128]{3,2,0,1:T(8,128)(2,1)}) async-done(((bf16[64,1,128,128]{3,2,0,1:T(8,128)(2,1)}, bf16[64,1,128,128]{3,2,0,1:T(8,128)(2,1)}), (bf16[64,1,128,128]{3,2,0,1:T(8,128)(2,1)}, bf16[64,1,128,128]{3,2,0,1:T(8,128)(2,1)})) %all-reduce.4.cloned.1.call-update) | async-done | bytes 4194320 | tf_op jit(solution)/shard_map/psum | solution.py:125
  281.1 60.5 %all_to_all.41 = bf16[64,1,128,128]{3,2,1,0:T(8,128)(2,1)} all-to-all(bf16[64,1,128,128]{3,2,1,0:T(8,128)(2,1)} %bitcast.134), channel_id=1, replica_groups=mesh['dp'=4,'mem'=64] {'mem'}, dimensions={0} | all-to-all | bytes 4194304 | tf_op jit(solution)/shard_map/all_to_all | solution.py:139
  341.6 7.4 %all-to-all-start.5 = ((bf16[64,1,128,128]{3,2,1,0:T(8,128)(2,1)}), bf16[64,1,128,128]{3,2,1,0:T(8,128)(2,1)}, u32[]{:S(2)}, u32[]{:S(2)}) async-start(bf16[64,1,128,128]{3,2,1,0:T(8,128)(2,1)} %bitcast.133), calls=%async_computation.5 | async-start | bytes 4194304 | tf_op jit(solution)/shard_map/all_to_all | solution.py:140
  348.9 1.1 copy.101
  350.1 2.0 copy.102
  352.0 2.0 copy.100
  354.1 1.2 copy.95
  355.3 1.5 fusion.11
  356.9 1.0 copy-done.5
  357.9 0.2 fusion.56
  358.1 3.2 fusion.13
  361.3 1.2 reduce.8
  362.5 4.3 gather_fusion.2
  366.8 4.3 gather_fusion.4
  371.2 2.3 fusion.16
  373.5 1.9 copy-done.2
  375.4 1.1 fusion.57
  376.6 7.3 %fusion.12 = (f32[16]{0:T(128)S(1)}, f32[16,128,128]{1,2,0:T(8,128)}) fusion(f32[1,16,128,128]{2,3,1,0:T(8,128)} %bitcast.138, f32[16,128,128]{1,2,0:T(8,128)S(1)} %copy-done.4, bf16[16,512,128]{2,1,0:T(8,128)(2,1)} %bitcast.135, f32[16,128]{1,0:T(8,128)S(1)} %fusion.57, f32[16,512,128]{2,1,0:T(8,128)} %copy-done.2), kind=kOutput, calls=%fused_computation.29 | convolution fusion | flops 274467328 | bytes 9445440 | tf_op jit(solution)/shard_map/thqk,thkd->thqd/dot_general | solution.py:18
  384.0 76.4 %psum.23 = f32[16]{0:T(128)S(1)} all-reduce(f32[16]{0:T(128)S(1)} %get-tuple-element.38), channel_id=1, replica_groups=mesh['dp'=4,'mem'=64] {'dp','mem'}, use_global_device_ids=true, to_apply=%region_15.16 | all-reduce | flops 16 | bytes 128 | tf_op jit(solution)/shard_map/psum | solution.py:108
  460.3 0.5 multiply_multiply_fusion
  460.9 1.8 add_convert_fusion
  462.6 1.0 copy.96
  463.6 9.3 %scatter_fusion.1 = bf16[64,128,128]{2,1,0:T(8,128)(2,1)} fusion(bf16[64,128,128]{2,1,0:T(8,128)(2,1)} %bitcast.126, s32[64]{0:T(128)S(1)} %fusion.47, bf16[64,128,128]{2,1,0:T(8,128)(2,1)} %bitcast.130), kind=kCustom, calls=%fused_computation.9 | custom fusion | bytes 6291712 | tf_op jit(solution)/shard_map/scatter | solution.py:30
  473.0 6.6 %scatter_fusion.3 = bf16[64,128,128]{2,1,0:T(8,128)(2,1)S(1)} fusion(bf16[64,128,128]{2,1,0:T(8,128)(2,1)S(1)} %bitcast.123, s32[64]{0:T(128)S(1)} %fusion.47, bf16[64,128,128]{2,1,0:T(8,128)(2,1)} %bitcast.38), kind=kCustom, calls=%fused_computation.11 | custom fusion | bytes 6291712 | tf_op jit(solution)/shard_map/scatter | solution.py:30
  479.6 1.3 copy-done.1
  (57 shorter events, 1.6 us)
Async XLA Ops:
  7.2 3.8 copy-start
  7.2 3.3 copy-start.3
  7.2 3.5 copy-start.9
  11.0 15.8 %copy-start.11 = (s32[8]{0:T(128)S(1)}, s32[8]{0:T(128)}, u32[]{:S(2)}) copy-start(s32[8]{0:T(128)} %param.23) | copy-start | bytes 100
  11.0 16.5 %copy-start.12 = (u32[256]{0:T(256)S(1)}, u32[256]{0:T(256)}, u32[]{:S(2)}) copy-start(u32[256]{0:T(256)} %constant.158) | copy-start | bytes 3076
  13.7 24.3 %all-to-all-start = ((s32[64,1,2]{2,1,0:T(1,128)}), s32[64,1,2]{2,1,0:T(1,128)S(1)}, u32[]{:S(2)}, u32[]{:S(2)}) async-start(s32[64,1,2]{2,1,0:T(1,128)} %bitcast.6), calls=%async_computation | async-start | bytes 65536 | tf_op jit(solution)/shard_map/all_to_all | solution.py:75
  37.9 21.0 %all-to-all-start.3 = ((s32[64,1,1]{2,1,0:T(1,128)}), s32[64,1,1]{2,1,0:T(1,128)S(1)}, u32[]{:S(2)}, u32[]{:S(2)}) async-start(s32[64,1,1]{2,1,0:T(1,128)} %copy.92), calls=%async_computation.3 | async-start | bytes 65536 | tf_op jit(solution)/shard_map/all_to_all | solution.py:141
  59.0 100.6 %all-to-all-start.1 = ((bf16[64,2,128,128]{3,2,1,0:T(8,128)(2,1)}), bf16[64,2,128,128]{3,2,1,0:T(8,128)(2,1)}, u32[]{:S(2)}, u32[]{:S(2)}) async-start(bf16[64,2,128,128]{3,2,1,0:T(8,128)(2,1)} %bitcast.129), calls=%async_computation.1 | async-start | bytes 8388608 | tf_op jit(solution)/shard_map/all_to_all | solution.py:79
  159.6 7.6 %copy-start.7 = (bf16[8,128,128]{2,1,0:T(8,128)(2,1)S(1)}, bf16[8,128,128]{2,1,0:T(8,128)(2,1)}, u32[]{:S(2)}) copy-start(bf16[8,128,128]{2,1,0:T(8,128)(2,1)} %param.17) | copy-start | bytes 786436
  159.6 7.6 %copy-start.8 = (bf16[8,128,128]{2,1,0:T(8,128)(2,1)S(1)}, bf16[8,128,128]{2,1,0:T(8,128)(2,1)}, u32[]{:S(2)}) copy-start(bf16[8,128,128]{2,1,0:T(8,128)(2,1)} %param.18) | copy-start | bytes 786436
  159.6 121.5 %all-to-all-start.2 = ((bf16[64,2,128,128]{3,2,1,0:T(8,128)(2,1)}), bf16[64,2,128,128]{3,2,1,0:T(8,128)(2,1)}, u32[]{:S(2)}, u32[]{:S(2)}) async-start(bf16[64,2,128,128]{3,2,1,0:T(8,128)(2,1)} %bitcast.128), calls=%async_computation.2 | async-start | bytes 8388608 | tf_op jit(solution)/shard_map/all_to_all | solution.py:80
  167.1 114.0 %all-reduce.4.cloned.1.call-start = ((), (), s32[]{:S(2)}) async-start(), calls=%async_computation.6 | async-start | bytes 8388608 | tf_op jit(solution)/shard_map/psum | solution.py:125
  341.6 12.5 %copy-start.6 = (bf16[128,2048]{1,0:T(8,128)(2,1)S(1)}, bf16[128,2048]{1,0:T(8,128)(2,1)}, u32[]{:S(2)}) copy-start(bf16[128,2048]{1,0:T(8,128)(2,1)} %param.20) | copy-start | bytes 1572868
  341.6 131.4 %all-to-all-start.5 = ((bf16[64,1,128,128]{3,2,1,0:T(8,128)(2,1)}), bf16[64,1,128,128]{3,2,1,0:T(8,128)(2,1)}, u32[]{:S(2)}, u32[]{:S(2)}) async-start(bf16[64,1,128,128]{3,2,1,0:T(8,128)(2,1)} %bitcast.133), calls=%async_computation.5 | async-start | bytes 4194304 | tf_op jit(solution)/shard_map/all_to_all | solution.py:140
  356.9 1.0 copy-start.5
  373.5 1.9 copy-start.2
  375.4 1.2 copy-start.4
  376.6 83.7 %copy-start.10 = (f32[16]{0:T(128)S(1)}, f32[16]{0:T(128)}, u32[]{:S(2)}) copy-start(f32[16]{0:T(128)} %param.19) | copy-start | bytes 196
  479.6 1.3 copy-start.1
Sparse Core Ops, SparseCore 0:
  183.8 97.2 all-reduce.3
where the time goes:
time: 489 us; the launch traced here: 488 us
  waiting for transfers between devices  193 us (39%)
  blocking collectives  144 us (29%)
  local copies, waits for them, and re-layouts  63 us (13%)
  starting transfers between devices  46 us (9%)
  between operations  15 us (3%)
  matrix products  14.4 us (3%)
  other arithmetic  12 us (2%)
    psum x1, waiting for transfers between devices, on_device(): lax.psum(own_keys.astype(jnp.bfloat16), 'dp').astype(jnp.float32)  97.4 us
    all_to_all x1, waiting for transfers between devices, on_device(): lax.all_to_all(flat_keys[clipped], 'mem', split_axis=0, concat_axis=0, ti...  91.3 us
    psum x1, blocking collectives, on_device(): grad_total = lax.psum(partial_value, ('dp', 'mem'))  76.4 us
    all_to_all x1, blocking collectives, on_device(): lax.all_to_all(box_keys, 'mem', split_axis=0, concat_axis=0, tiled=True)  60.5 us
    scatter x2, local copies, waits for them, and re-layouts, apply_writes(): flat.at[target].set(payload.reshape((-1,) + flat.shape[1:]), mode='drop')  16 us
    all_to_all x1, starting transfers between devices, on_device(): lax.all_to_all(request_box, 'mem', split_axis=0, concat_axis=0, tiled=True)  13.2 us
    unnamed x33, local copies, waits for them, and re-layouts  12.5 us
    all_to_all x1, starting transfers between devices, on_device(): lax.all_to_all(box_codes, 'mem', split_axis=0, concat_axis=0, tiled=True)  11.7 us
  transfers between devices with their start and end apart: 6, of which 3 were waited for; matrix products, arithmetic and copies ran while one was open for 15% of the time, Pallas kernels for 0%

commit v1 on v0

v1 whole, which is shorter than its diff:
```python
import functools
import math

import jax
import jax.numpy as jnp
from jax import lax
from jax.experimental import pallas as pl
from jax.experimental.pallas import tpu as pltpu
from jax.sharding import PartitionSpec as P

MESH = pl.DeviceIdType.MESH
BF16, F32 = jnp.bfloat16, jnp.float32
NZ, NL, ND = 8, 8, 4
OFFSETS = (3, -4, 2, -3, 1, -2, -1, 0)
NONE = -1e30


def wrap(value, size):
    return lax.rem(value + 4 * size, size)


def codes(block_home, query_blocks, write_slots):
    group, place = lax.axis_index("dp"), lax.axis_index("mem")
    layer, lane = place // NL, place % NL
    row = lane // 2
    lanes = jnp.arange(256, dtype=jnp.int32)
    wanted = query_blocks.reshape(16, 4)
    storage = jnp.sum(
        jnp.where(wanted[:, :, None] == lanes, block_home[:, None, :], 0), axis=-1
    ).reshape(64)
    owner = storage // 4
    count = jnp.arange(64, dtype=jnp.int32)
    rank = jnp.sum(
        ((owner[:, None] == owner[None, :]) & (count[:, None] > count[None, :])).astype(jnp.int32),
        axis=1,
    )
    homes = lax.dynamic_slice_in_dim(block_home, (place % 2) * 8, 8, 0)
    written = jnp.sum(jnp.where(write_slots[:, None] == lanes, homes, 0), axis=-1)
    packed = jnp.concatenate([storage * 2 + rank, written])
    everyone = lax.all_gather(packed, ("dp", "mem"), axis=0, tiled=False).reshape(ND, 64, 72)

    asked = lax.dynamic_index_in_dim(everyone, group, 0, keepdims=False)[:, :64]
    request = count[None, :, None]
    slot = jnp.arange(2, dtype=jnp.int32)
    select = jnp.sum(
        jnp.where(
            (asked[:, :, None] // 8 == place) & (asked[:, :, None] % 2 == slot),
            (asked[:, :, None] // 2 % 4) * 16 + request // 4,
            0,
        ),
        axis=1,
    ).reshape(128)
    column = lax.dynamic_index_in_dim(asked.reshape(NZ, NL, 64), lane, 1, keepdims=False)
    found = jnp.where(column // 64 == layer, (column // 8) % 8 * 2 + column % 2, -1)
    sixteen = jnp.arange(16, dtype=jnp.int32)
    heads = jnp.sum(
        jnp.where(found[:, :, None] == sixteen, request // 4, 0), axis=1
    ).reshape(128)

    targets = everyone[:, :, 64:]
    units = lax.dynamic_index_in_dim(targets, place, 1, keepdims=False).reshape(32)
    to_row = (row + group + layer) % 4
    to = sixteen // 2 * NL + to_row * 2 + sixteen % 2
    send = jnp.sum(
        jnp.where(units[None, :] // 4 == to[:, None], jnp.arange(32, dtype=jnp.int32), 0), axis=1
    )
    source = jnp.arange(64, dtype=jnp.int32)
    via = (row - source % NL // 2 - source // NL + 16) % 4
    landing = (via * NL + source % NL) * 2 + source // NL // 4
    unit_head = (source[:, None] * 8 + jnp.arange(8, dtype=jnp.int32)) % 16
    slab = jnp.where(targets // 4 == place, targets % 4 * 16 + unit_head, -1)
    come = jnp.max(slab, axis=(0, 2))
    fetch = jnp.max(
        jnp.where(come[None, :] == source[:, None], landing[None, :], -1), axis=1
    )
    return select, heads, found.reshape(512), send, fetch


def kernel(
    select,
    heads,
    found,
    send,
    fetch,
    gate,
    q_ref,
    kl_ref,
    vl_ref,
    cot_ref,
    mk_ref,
    mv_ref,
    pk_ref,
    pv_ref,
    mixed_ref,
    nk_ref,
    nv_ref,
    part_ref,
    kv_out,
    kv_in,
    q_all,
    slot_o,
    slot_s,
    near_o,
    res_o,
    res_s,
    got_o,
    got_s,
    unit_all,
    w_out,
    w_mid,
    w_in,
    bar_unused,
    kv_send,
    kv_recv,
    q_send,
    q_recv,
    ro_send,
    ro_recv,
    rs_send,
    rs_recv,
    x_send,
    x_recv,
    wz_send,
    wz_recv,
    wy_send,
    wy_recv,
    wx_send,
    wx_recv,
):
    group, place = lax.axis_index("dp"), lax.axis_index("mem")
    layer, lane = lax.div(place, NL), lax.rem(place, NL)
    row = lax.div(lane, 2)
    scale = 1.0 / math.sqrt(128.0)

    def at(g, z, l):
        return (g, z * NL + l)

    def remote(src, dst, s, r, to):
        return pltpu.make_async_remote_copy(
            src_ref=src, dst_ref=dst, send_sem=s, recv_sem=r, device_id=to, device_id_type=MESH
        )

    barrier = pltpu.get_barrier_semaphore()

    @pl.loop(1, 8)
    def _(r):
        pl.semaphore_signal(barrier, inc=1, device_id=at(group, layer, wrap(lane + r, NL)), device_id_type=MESH)
        pl.semaphore_signal(barrier, inc=1, device_id=at(group, wrap(layer + r, NZ), lane), device_id_type=MESH)

    @pl.loop(1, 4)
    def _(r):
        pl.semaphore_signal(barrier, inc=1, device_id=at(wrap(group + r, ND), layer, lane), device_id_type=MESH)

    for h in range(16):
        q_all[layer, h] = q_ref[:, h * 128 : (h + 1) * 128]
    for u in range(8):
        unit_all[group, u, 0] = pk_ref[u]
        unit_all[group, u, 1] = pv_ref[u]
    pl.semaphore_wait(barrier, 17)

    def q_copy(hop, up):
        source = wrap(layer - hop if up else layer + hop, NZ)
        to = at(group, wrap(layer + (1 if up else -1), NZ), lane)
        k = 0 if up else 1
        return remote(
            q_all.at[source], q_all.at[source], q_send.at[k, hop], q_recv.at[k, hop], to
        )

    q_copy(0, True).start()
    q_copy(0, False).start()

    def x_copy(r):
        return remote(
            unit_all.at[group],
            unit_all.at[group],
            x_send.at[r],
            x_recv.at[r],
            at(wrap(group + r, ND), layer, lane),
        )

    @pl.loop(1, 4)
    def _(r):
        x_copy(r).start()

    def kv_copy(i, r):
        return remote(
            kv_out.at[i, r],
            kv_in.at[i, lane],
            kv_send.at[i, r],
            kv_recv.at[i, r],
            at(group, layer, wrap(lane + r, NL)),
        )

    for i, off in enumerate(OFFSETS):
        tile = wrap(layer + off, NZ)
        for k in range(2):
            code = select[(tile * NL + lane) * 2 + k]
            kv_in[i, lane, 0, k] = mk_ref[code]
            kv_in[i, lane, 1, k] = mv_ref[code]

        @pl.loop(1, 8)
        def _(r):
            for k in range(2):
                code = select[(tile * NL + wrap(lane + r, NL)) * 2 + k]
                kv_out[i, r, 0, k] = mk_ref[code]
                kv_out[i, r, 1, k] = mv_ref[code]
            kv_copy(i, r).start()

    def attend(qh, kh, vh, allowed=None):
        scores = (
            lax.dot_general(qh, kh, (((1,), (1,)), ((), ())), preferred_element_type=F32) * scale
        )
        if allowed is not None:
            scores = jnp.where(allowed, scores, NONE)
        top = jnp.max(scores, axis=1, keepdims=True)
        shifted = jnp.exp(scores - top)
        total = jnp.sum(shifted, axis=1, keepdims=True)
        out = jnp.dot(shifted.astype(BF16), vh, preferred_element_type=F32) / total
        return out, top + jnp.log(total)

    rows_at = lax.broadcasted_iota(jnp.int32, (128, 128), 0)
    cols_at = lax.broadcasted_iota(jnp.int32, (128, 128), 1)

    def near(first):
        @pl.loop(first, first + 8)
        def _(h):
            cols = pl.ds(pl.multiple_of(h * 128, 128), 128)
            out, _ = attend(q_ref[:, cols], kl_ref[:, cols], vl_ref[:, cols], rows_at >= cols_at)
            near_o[h] = out

    near(0)
    for hop in range(4):
        q_copy(hop, True).wait_recv()
        if hop < 3:
            q_copy(hop + 1, True).start()
            q_copy(hop, False).wait_recv()
        if hop < 2:
            q_copy(hop + 1, False).start()
        if hop == 0:
            near(8)
        if hop == 1:
            @pl.loop(1, 4)
            def _(r):
                x_copy(r).wait_recv()

            for r in range(8):
                to_layer = wrap(layer + r, NZ)
                for k in range(2):
                    unit = send[to_layer * 2 + k]
                    for kv in range(2):
                        slab = unit_all[unit // 8, unit % 8, kv]
                        if r == 0:
                            w_mid[k, lax.rem(layer, 4), lax.div(layer, 4), kv] = slab
                        else:
                            w_out[r, k, kv] = slab
                    if r > 0:
                        wz_copy_args = (
                            w_out.at[r, k],
                            w_mid.at[k, lax.rem(layer, 4), lax.div(layer, 4)],
                            wz_send.at[r, k],
                            wz_recv.at[r, k],
                            at(group, to_layer, lane),
                        )
                        remote(*wz_copy_args).start()

    def wz_copy(r, k):
        return remote(
            w_out.at[r, k],
            w_mid.at[k, lax.rem(layer, 4), lax.div(layer, 4)],
            wz_send.at[r, k],
            wz_recv.at[r, k],
            at(group, wrap(layer + r, NZ), lane),
        )

    def wy_copy(r):
        peer = wrap(lane + r, NL)
        low = wrap(lax.div(peer, 2) - row - group, 4)
        return remote(
            w_mid.at[lax.rem(peer, 2), low],
            w_in.at[group, lane],
            wy_send.at[r],
            wy_recv.at[r],
            at(group, layer, peer),
        )

    def wx_copy(r):
        return remote(
            w_in.at[group],
            w_in.at[group],
            wx_send.at[r],
            wx_recv.at[r],
            at(wrap(group + r, ND), layer, lane),
        )

    def result_copies(i):
        to = at(group, wrap(layer + (1 if OFFSETS[i] > 0 else -1), NZ), lane)
        return (
            remote(res_o.at[i], got_o.at[i], ro_send.at[i], ro_recv.at[i], to),
            remote(res_s.at[i], got_s.at[i], rs_send.at[i], rs_recv.at[i], to),
        )

    joins = []
    for i, off in enumerate(OFFSETS):
        if off == 0:
            joins.append((OFFSETS.index(1), OFFSETS.index(-1)))
        else:
            further = off + (1 if off > 0 else -1)
            joins.append((OFFSETS.index(further),) if further in OFFSETS else ())

    for i, off in enumerate(OFFSETS):
        tile = wrap(layer + off, NZ)

        @pl.loop(1, 8)
        def _(r):
            kv_copy(i, r).wait_recv()

        @pl.loop(0, 4)
        def _(step):
            for k in range(4):
                s = step * 4 + k
                head = heads[tile * 16 + s]
                kh, vh = kv_in[i, step * 2 + k // 2, 0, k % 2], kv_in[i, step * 2 + k // 2, 1, k % 2]
                out, stat = attend(q_all[tile, head], kh, vh)
                slot_o[s] = out
                slot_s[s] = jnp.broadcast_to(stat, (128, 128))

        for j in joins[i]:
            for copy in result_copies(j):
                copy.wait_recv()
        if off != 0:
            res_s[i] = jnp.full((128, 128), NONE, F32)

        @pl.loop(0, 16)
        def _(h):
            outs, stats = [], []
            for j in range(4):
                where = found[tile * 64 + h * 4 + j]
                spot = jnp.maximum(where, 0)
                outs.append(slot_o[spot])
                stats.append(jnp.where(where >= 0, slot_s[spot], NONE))
            for j in joins[i]:
                outs.append(got_o[j, h].astype(F32))
                stat = jnp.sum(jnp.where(cols_at == h, got_s[j], 0.0), axis=1, keepdims=True)
                stats.append(jnp.broadcast_to(stat, (128, 128)))
            top = functools.reduce(jnp.maximum, stats)
            weights = [jnp.exp(stat - top) for stat in stats]
            total = functools.reduce(jnp.add, weights)
            out = functools.reduce(jnp.add, [w * o for w, o in zip(weights, outs)]) / total
            if off != 0:
                res_o[i, h] = out.astype(BF16)
                res_s[i] = jnp.where(cols_at == h, top + jnp.log(total), res_s[i])
            else:
                cols = pl.ds(pl.multiple_of(h * 128, 128), 128)
                opening = gate[h]
                local = near_o[h]
                mixed_ref[:, cols] = (opening * out + (1.0 - opening) * local).astype(BF16)
                part_ref[pl.ds(h, 1), :] = jnp.sum(
                    cot_ref[:, cols].astype(F32) * (out - local), axis=0, keepdims=True
                )

        if off != 0:
            for copy in result_copies(i):
                copy.start()
        if i == 1:
            @pl.loop(1, 8)
            def _(r):
                for k in range(2):
                    wz_copy(r, k).wait_recv()

            low = wrap(-group, 4)
            w_in[group, lane] = w_mid[lax.rem(lane, 2), low]

            @pl.loop(1, 8)
            def _(r):
                wy_copy(r).start()

        if i == 3:
            @pl.loop(1, 8)
            def _(r):
                wy_copy(r).wait_recv()

            @pl.loop(1, 4)
            def _(r):
                wx_copy(r).start()

    @pl.loop(1, 4)
    def _(r):
        wx_copy(r).wait_recv()

    @pl.loop(0, 64)
    def _(slab):
        where = fetch[slab]
        spot = jnp.maximum(where, 0)
        for kv, (old, new) in enumerate(((mk_ref, nk_ref), (mv_ref, nv_ref))):
            came = w_in[spot // 16, spot // 2 % 8, spot % 2, kv]
            new[slab] = jnp.where(where >= 0, came, old[slab])

    for hop in range(4):
        q_copy(hop, True).wait_send()
        if hop < 3:
            q_copy(hop, False).wait_send()
    for i, off in enumerate(OFFSETS):
        if off != 0:
            for copy in result_copies(i):
                copy.wait_send()

        @pl.loop(1, 8)
        def _(r):
            kv_copy(i, r).wait_send()

    @pl.loop(1, 4)
    def _(r):
        x_copy(r).wait_send()
        wx_copy(r).wait_send()

    @pl.loop(1, 8)
    def _(r):
        wy_copy(r).wait_send()
        for k in range(2):
            wz_copy(r, k).wait_send()


def on_device(
    queries,
    keys_local,
    values_local,
    mem_keys,
    mem_values,
    prev_keys,
    prev_values,
    gate_logit,
    cotangent,
    block_home,
    query_blocks,
    write_slots,
):
    tables = codes(block_home, query_blocks, write_slots)
    sigmoid_gate = jax.nn.sigmoid(gate_logit)
    smem, vmem = (pl.BlockSpec(memory_space=space) for space in (pltpu.SMEM, pltpu.VMEM))
    dma = pltpu.SemaphoreType.DMA
    mixed, new_keys, new_values, part = pl.pallas_call(
        kernel,
        out_shape=(
            jax.ShapeDtypeStruct((128, 2048), BF16),
            jax.ShapeDtypeStruct((64, 128, 128), BF16),
            jax.ShapeDtypeStruct((64, 128, 128), BF16),
            jax.ShapeDtypeStruct((16, 128), F32),
        ),
        in_specs=[smem] * 6 + [vmem] * 8,
        out_specs=(vmem,) * 4,
        scratch_shapes=[
            pltpu.VMEM((8, 8, 2, 2, 128, 128), BF16),
            pltpu.VMEM((8, 8, 2, 2, 128, 128), BF16),
            pltpu.VMEM((8, 16, 128, 128), BF16),
            pltpu.VMEM((16, 128, 128), F32),
            pltpu.VMEM((16, 128, 128), F32),
            pltpu.VMEM((16, 128, 128), F32),
            pltpu.VMEM((7, 16, 128, 128), BF16),
            pltpu.VMEM((7, 128, 128), F32),
            pltpu.VMEM((7, 16, 128, 128), BF16),
            pltpu.VMEM((7, 128, 128), F32),
            pltpu.VMEM((4, 8, 2, 128, 128), BF16),
            pltpu.VMEM((8, 2, 2, 128, 128), BF16),
            pltpu.VMEM((2, 4, 2, 2, 128, 128), BF16),
            pltpu.VMEM((4, 8, 2, 2, 128, 128), BF16),
            pltpu.SMEM((1,), jnp.int32),
            dma((8, 8)),
            dma((8, 8)),
            dma((2, 4)),
            dma((2, 4)),
            dma((7,)),
            dma((7,)),
            dma((7,)),
            dma((7,)),
            dma((4,)),
            dma((4,)),
            dma((8, 2)),
            dma((8, 2)),
            dma((8,)),
            dma((8,)),
            dma((4,)),
            dma((4,)),
        ],
        compiler_params=pltpu.CompilerParams(
            collective_id=0, has_side_effects=True, vmem_limit_bytes=60 * 1024 * 1024
        ),
    )(
        *tables,
        sigmoid_gate,
        queries,
        keys_local,
        values_local,
        cotangent,
        mem_keys.reshape(64, 128, 128),
        mem_values.reshape(64, 128, 128),
        prev_keys,
        prev_values,
    )
    total = lax.psum(jnp.sum(part, axis=1), ("dp", "mem"))
    gate_grad = sigmoid_gate * (1.0 - sigmoid_gate) * total
    return mixed, new_keys.reshape(mem_keys.shape), new_values.reshape(mem_values.shape), gate_grad


def solution(mesh):
    tokens, slabs = P(("dp", "mem"), None), P("mem", None, None, None)
    units = P(("dp", "mem"), None, None)
    return jax.shard_map(
        on_device,
        mesh=mesh,
        in_specs=(
            tokens,
            tokens,
            tokens,
            slabs,
            slabs,
            units,
            units,
            P(),
            tokens,
            P(),
            units,
            P(("dp", "mem")),
        ),
        out_specs=(tokens, slabs, slabs, P()),
        check_vma=False,
    )
```

time: 489 us -> 519 us (1.061)
  Pallas kernels: 0 us -> 163 us
  blocking collectives: 144 us -> 75.1 us
  waiting for transfers between devices: 193 us -> 247 us
  local copies, waits for them, and re-layouts: 63 us -> 11.1 us
  starting transfers between devices: 46 us -> 0.04 us
  matrix products: 14.4 us -> 0 us
    unnamed x1 -> x2, waiting for transfers between devices: 0.02 us -> 247 us
    pallas_call x0 -> x1, Pallas kernels: none -> 163 us  [on_device(): pl.pallas_call(kernel, out_shape=(jax.ShapeDtypeStruct((128, 2048), BF16)...]
    psum x1 -> x0, waiting for transfers between devices: 97.4 us -> none  [on_device(): lax.psum(own_keys.astype(jnp.bfloat16), 'dp').astype(jnp.float32)]
    all_to_all x5 -> x0, waiting for transfers between devices: 95.7 us -> none  [the longest x1 91.3 us: on_device(): lax.all_to_all(flat_keys[clipped], 'mem', split_axis=0, concat_axis=0, ti...]
    all_to_all x1 -> x0, blocking collectives: 60.5 us -> none  [on_device(): lax.all_to_all(box_keys, 'mem', split_axis=0, concat_axis=0, tiled=True)]
    all_to_all x5 -> x0, starting transfers between devices: 45.9 us -> none  [the longest x1 13.2 us: on_device(): lax.all_to_all(request_box, 'mem', split_axis=0, concat_axis=0, tiled=True)]
    scatter x6 -> x0, local copies, waits for them, and re-layouts: 22.3 us -> none  [the longest x2 16 us: apply_writes(): flat.at[target].set(payload.reshape((-1,) + flat.shape[1:]), mode='drop')]
    gather x6 -> x0, local copies, waits for them, and re-layouts: 17.9 us -> none  [the longest x1 4.65 us: on_device(): flat_keys[clipped]]
  transfers between devices with their start and end apart: 6 -> 1, of which waited for: 3 -> 1; matrix products, arithmetic and copies ran while one was open for 15% -> 0% of each run, Pallas kernels for 0% -> 0%
where the time goes in v1:
time: 519 us; the launch traced here: 518 us
  waiting for transfers between devices  247 us (48%)
  Pallas kernels  163 us (31%)
  blocking collectives  75.1 us (14%)
  between operations  14.3 us (3%)
  local copies, waits for them, and re-layouts  11.1 us (2%)
  other arithmetic  7.63 us (1%)
    unnamed x2, waiting for transfers between devices  247 us
    pallas_call x1, Pallas kernels, on_device(): pl.pallas_call(kernel, out_shape=(jax.ShapeDtypeStruct((128, 2048), BF16)...  163 us
    psum x1, blocking collectives, on_device(): total = lax.psum(jnp.sum(part, axis=1), ('dp', 'mem'))  75.1 us
  transfers between devices with their start and end apart: 1, of which 1 were waited for; matrix products, arithmetic and copies ran while one was open for 0% of the time, Pallas kernels for 0%

profile of v1, /device:TPU:1, one launch (start us, length us, event | category | flops | bytes accessed | tf_op | source)
XLA Modules:
  0.0 518.5 jit_solution(5187787492321455111)
XLA Ops:
  7.2 0.0 all-reduce.3.cloned.1.call-start
  7.3 0.9 select_reduce_fusion.2
  8.2 0.1 copy.18
  8.3 0.1 reshape.438
  8.4 0.2 convert_reduce_fusion
  8.6 0.9 select_reduce_fusion.5
  9.5 0.2 add_dynamic-update-slice_fusion
  9.7 0.0 copy-start.1
  9.7 0.6 copy-done.1
  10.3 0.0 all-reduce.3.cloned.1.call-update
  10.4 1.2 add_divide_fusion.gate
  11.7 0.1 add_select_fusion.2
  11.8 246.9 %all-reduce.3.cloned.1.call-done = s32[18432]{0:T(1024)} async-done(((s32[18432]{0:T(1024)}), s32[18432]{0:T(1024)}) %all-reduce.3.cloned.1.call-update) | async-done | bytes 73744
  258.7 1.0 reshape.439
  259.8 0.3 fusion.4
  260.2 0.1 broadcast_in_dim_reshape.4
  260.3 0.5 broadcast.647
  260.8 0.7 fusion.46
  261.5 0.1 squeeze.14
  261.6 0.6 fusion.36.found
  262.2 0.2 select_reduce_fusion
  262.4 0.6 reshape.442.heads
  263.0 0.1 select_reduce_fusion.1
  263.1 0.1 copy.19
  263.2 0.7 reshape.440.select
  263.9 0.7 select_reduce_fusion.3.fetch
  264.6 0.7 select_reduce_fusion.4.send
  265.3 0.0 copy-start.2
  265.3 163.4 %shard_map.147 = (bf16[128,2048]{1,0:T(8,128)(2,1)}, bf16[64,128,128]{2,1,0:T(8,128)(2,1)}, bf16[64,128,128]{2,1,0:T(8,128)(2,1)}, f32[16,128]{1,0:T(8,128)}) custom-call(s32[128]{0:T(128)} %reshape.440.select, s32[128]{0:T(128)} %reshape.442.heads, s32[512]{0:T(512)} %fusion.36.found, s32[16]{0:T(128)} %select_reduce_fusion.4.send, ...), custom_call_target="tpu_custom_call" | custom-call | tf_op jit(solution)/shard_map/pallas_call | solution.py:441
  428.7 0.8 reduce_sum.69
  429.5 75.1 %psum.7 = f32[16]{0:T(128)S(1)} all-reduce(f32[16]{0:T(128)S(1)} %reduce_sum.69), channel_id=1, replica_groups=mesh['dp'=4,'mem'=64] {'dp','mem'}, use_global_device_ids=true, to_apply=%region_9.10 | all-reduce | flops 16 | bytes 128 | tf_op jit(solution)/shard_map/psum | solution.py:499
  504.6 0.0 copy-done.2
  504.6 0.5 fusion.39
  505.1 1.9 copy.25
  507.0 0.0 copy-start
  507.0 3.3 copy.26
  510.3 0.0 copy-done
  510.3 1.3 copy.27
  (13 shorter events, 0.2 us)
Async XLA Ops:
  7.2 251.6 %all-reduce.3.cloned.1.call-start = ((), (), s32[]{:S(2)}) async-start(), calls=%async_computation | async-start | bytes 147456
  9.7 0.6 copy-start.1
  265.3 239.3 %copy-start.2 = (f32[16]{0:T(128)S(1)}, f32[16]{0:T(128)}, u32[]{:S(2)}) copy-start(f32[16]{0:T(128)} %param.19) | copy-start | bytes 196
  507.0 3.3 copy-start
Sparse Core Ops, SparseCore 0:
  14.1 244.5 all-reduce.2

commit v2 on v1

--- a/solution.py
+++ b/solution.py
@@ -17,6 +17,67 @@
 
 def wrap(value, size):
     return lax.rem(value + 4 * size, size)
+
+
+def peers(group, layer, lane):
+    in_layer = lambda r: (group, layer * NL + wrap(lane + r, NL))
+    along_z = lambda r: (group, wrap(layer + r, NZ) * NL + lane)
+    in_groups = lambda r: (wrap(group + r, ND), layer * NL + lane)
+    return in_layer, along_z, in_groups
+
+
+def greet(group, layer, lane):
+    barrier = pltpu.get_barrier_semaphore()
+    in_layer, along_z, in_groups = peers(group, layer, lane)
+
+    @pl.loop(1, 8)
+    def _(r):
+        pl.semaphore_signal(barrier, inc=1, device_id=in_layer(r), device_id_type=MESH)
+        pl.semaphore_signal(barrier, inc=1, device_id=along_z(r), device_id_type=MESH)
+
+    @pl.loop(1, 4)
+    def _(r):
+        pl.semaphore_signal(barrier, inc=1, device_id=in_groups(r), device_id_type=MESH)
+
+    return lambda: pl.semaphore_wait(barrier, 17)
+
+
+def remote(src, dst, s, r, to):
+    return pltpu.make_async_remote_copy(
+        src_ref=src, dst_ref=dst, send_sem=s, recv_sem=r, device_id=to, device_id_type=MESH
+    )
+
+
+def code_kernel(own, out, x_send, x_recv, l_send, l_recv, z_send, z_recv):
+    group, place = lax.axis_index("dp"), lax.axis_index("mem")
+    layer, lane = lax.div(place, NL), lax.rem(place, NL)
+    in_layer, along_z, in_groups = peers(group, layer, lane)
+    ready = greet(group, layer, lane)
+    out[layer, lane, group] = own[...]
+    ready()
+    for part, size, s, r, to in (
+        (out.at[layer, lane, group], ND, x_send, x_recv, in_groups),
+        (out.at[layer, lane], NL, l_send, l_recv, in_layer),
+        (out.at[layer], NZ, z_send, z_recv, along_z),
+    ):
+        copies = [remote(part, part, s.at[k], r.at[k], to(k)) for k in range(1, size)]
+        for copy in copies:
+            copy.start()
+        for copy in copies:
+            copy.wait()
+
+
+def gather_codes(own):
+    dma = pltpu.SemaphoreType.DMA
+    vmem = pl.BlockSpec(memory_space=pltpu.VMEM)
+    return pl.pallas_call(
+        code_kernel,
+        out_shape=jax.ShapeDtypeStruct((NZ, NL, ND, 1, 128), jnp.int32),
+        in_specs=[vmem],
+        out_specs=vmem,
+        scratch_shapes=[dma((ND,)), dma((ND,)), dma((NL,)), dma((NL,)), dma((NZ,)), dma((NZ,))],
+        compiler_params=pltpu.CompilerParams(collective_id=1, has_side_effects=True),
+    )(own)
 
 
 def codes(block_home, query_blocks, write_slots):
@@ -36,8 +97,9 @@
     )
     homes = lax.dynamic_slice_in_dim(block_home, (place % 2) * 8, 8, 0)
     written = jnp.sum(jnp.where(write_slots[:, None] == lanes, homes, 0), axis=-1)
-    packed = jnp.concatenate([storage * 2 + rank, written])
-    everyone = lax.all_gather(packed, ("dp", "mem"), axis=0, tiled=False).reshape(ND, 64, 72)
+    packed = jnp.concatenate([storage * 2 + rank, written, jnp.zeros((56,), jnp.int32)])
+    everyone = gather_codes(packed.reshape(1, 128)).reshape(64, ND, 128)[:, :, :72]
+    everyone = everyone.transpose(1, 0, 2)
 
     asked = lax.dynamic_index_in_dim(everyone, group, 0, keepdims=False)[:, :64]
     request = count[None, :, None]
@@ -109,7 +171,10 @@
     w_out,
     w_mid,
     w_in,
-    bar_unused,
+    part,
+    g_x,
+    g_l,
+    g_z,
     kv_send,
     kv_recv,
     q_send,
@@ -126,6 +191,12 @@
     wy_recv,
     wx_send,
     wx_recv,
+    gx_send,
+    gx_recv,
+    gl_send,
+    gl_recv,
+    gz_send,
+    gz_recv,
 ):
     group, place = lax.axis_index("dp"), lax.axis_index("mem")
     layer, lane = lax.div(place, NL), lax.rem(place, NL)
@@ -135,28 +206,13 @@
     def at(g, z, l):
         return (g, z * NL + l)
 
-    def remote(src, dst, s, r, to):
-        return pltpu.make_async_remote_copy(
-            src_ref=src, dst_ref=dst, send_sem=s, recv_sem=r, device_id=to, device_id_type=MESH
-        )
-
-    barrier = pltpu.get_barrier_semaphore()
-
-    @pl.loop(1, 8)
-    def _(r):
-        pl.semaphore_signal(barrier, inc=1, device_id=at(group, layer, wrap(lane + r, NL)), device_id_type=MESH)
-        pl.semaphore_signal(barrier, inc=1, device_id=at(group, wrap(layer + r, NZ), lane), device_id_type=MESH)
-
-    @pl.loop(1, 4)
-    def _(r):
-        pl.semaphore_signal(barrier, inc=1, device_id=at(wrap(group + r, ND), layer, lane), device_id_type=MESH)
-
+    ready = greet(group, layer, lane)
     for h in range(16):
         q_all[layer, h] = q_ref[:, h * 128 : (h + 1) * 128]
     for u in range(8):
         unit_all[group, u, 0] = pk_ref[u]
         unit_all[group, u, 1] = pv_ref[u]
-    pl.semaphore_wait(barrier, 17)
+    ready()
 
     def q_copy(hop, up):
         source = wrap(layer - hop if up else layer + hop, NZ)
@@ -354,7 +410,7 @@
                 opening = gate[h]
                 local = near_o[h]
                 mixed_ref[:, cols] = (opening * out + (1.0 - opening) * local).astype(BF16)
-                part_ref[pl.ds(h, 1), :] = jnp.sum(
+                part[pl.ds(h, 1), :] = jnp.sum(
                     cot_ref[:, cols].astype(F32) * (out - local), axis=0, keepdims=True
                 )
 
@@ -383,9 +439,29 @@
             def _(r):
                 wx_copy(r).start()
 
+    in_layer, along_z, in_groups = peers(group, layer, lane)
+
+    def spread(value, held, mine, size, s, r, to):
+        held[mine] = value
+        copies = [
+            remote(held.at[mine], held.at[mine], s.at[k], r.at[k], to(k)) for k in range(1, size)
+        ]
+        for copy in copies:
+            copy.start()
+        return copies
+
+    def total_of(held, copies):
+        for copy in copies:
+            copy.wait()
+        return jnp.sum(held[...], axis=0)
+
+    gx = spread(part[...], g_x, group, ND, gx_send, gx_recv, in_groups)
+
     @pl.loop(1, 4)
     def _(r):
         wx_copy(r).wait_recv()
+
+    gl = spread(total_of(g_x, gx), g_l, lane, NL, gl_send, gl_recv, in_layer)
 
     @pl.loop(0, 64)
     def _(slab):
@@ -394,6 +470,8 @@
         for kv, (old, new) in enumerate(((mk_ref, nk_ref), (mv_ref, nv_ref))):
             came = w_in[spot // 16, spot // 2 % 8, spot % 2, kv]
             new[slab] = jnp.where(where >= 0, came, old[slab])
+
+    gz = spread(total_of(g_l, gl), g_z, layer, NZ, gz_send, gz_recv, along_z)
 
     for hop in range(4):
         q_copy(hop, True).wait_send()
@@ -418,6 +496,8 @@
         wy_copy(r).wait_send()
         for k in range(2):
             wz_copy(r, k).wait_send()
+
+    part_ref[...] = total_of(g_z, gz)
 
 
 def on_device(
@@ -463,7 +543,10 @@
             pltpu.VMEM((8, 2, 2, 128, 128), BF16),
             pltpu.VMEM((2, 4, 2, 2, 128, 128), BF16),
             pltpu.VMEM((4, 8, 2, 2, 128, 128), BF16),
-            pltpu.SMEM((1,), jnp.int32),
+            pltpu.VMEM((16, 128), F32),
+            pltpu.VMEM((ND, 16, 128), F32),
+            pltpu.VMEM((NL, 16, 128), F32),
+            pltpu.VMEM((NZ, 16, 128), F32),
             dma((8, 8)),
             dma((8, 8)),
             dma((2, 4)),
@@ -480,6 +563,12 @@
             dma((8,)),
             dma((4,)),
             dma((4,)),
+            dma((ND,)),
+            dma((ND,)),
+            dma((NL,)),
+            dma((NL,)),
+            dma((NZ,)),
+            dma((NZ,)),
         ],
         compiler_params=pltpu.CompilerParams(
             collective_id=0, has_side_effects=True, vmem_limit_bytes=60 * 1024 * 1024
@@ -496,7 +585,7 @@
         prev_keys,
         prev_values,
     )
-    total = lax.psum(jnp.sum(part, axis=1), ("dp", "mem"))
+    total = jnp.sum(part, axis=1)
     gate_grad = sigmoid_gate * (1.0 - sigmoid_gate) * total
     return mixed, new_keys.reshape(mem_keys.shape), new_values.reshape(mem_values.shape), gate_grad
 

time: 519 us -> 218 us (0.42)
  waiting for transfers between devices: 247 us -> 0 us
  blocking collectives: 75.1 us -> 0 us
  Pallas kernels: 163 us -> 197 us
  between operations: 14.3 us -> 0.83 us
    unnamed x2 -> x0, waiting for transfers between devices: 247 us -> none
    psum x1 -> x0, blocking collectives: 75.1 us -> none  [on_device(): total = lax.psum(jnp.sum(part, axis=1), ('dp', 'mem'))]
    pallas_call x0 -> x1, Pallas kernels: none -> 23.8 us  [gather_codes(): pl.pallas_call(code_kernel, out_shape=jax.ShapeDtypeStruct((NZ, NL, ND, 1...]
    pallas_call x1, Pallas kernels: 163 us -> 174 us  [on_device(): pl.pallas_call(kernel, out_shape=(jax.ShapeDtypeStruct((128, 2048), BF16)...]
  transfers between devices with their start and end apart: 1 -> 0, of which waited for: 1 -> 0; matrix products, arithmetic and copies ran while one was open for 0% -> 0% of each run, Pallas kernels for 0% -> 0%
where the time goes in v2:
time: 218 us
  Pallas kernels  197 us (90%)
  local copies, waits for them, and re-layouts  10.4 us (5%)
  other arithmetic  9.2 us (4%)
    pallas_call x1, Pallas kernels, on_device(): pl.pallas_call(kernel, out_shape=(jax.ShapeDtypeStruct((128, 2048), BF16)...  174 us
    pallas_call x1, Pallas kernels, gather_codes(): pl.pallas_call(code_kernel, out_shape=jax.ShapeDtypeStruct((NZ, NL, ND, 1...  23.8 us
    unnamed x7, local copies, waits for them, and re-layouts  6.51 us

profile of v2, /device:TPU:1, one launch (start us, length us, event | category | flops | bytes accessed | tf_op | source)
XLA Modules:
  0.0 217.8 jit_solution(7514859794143381056)
XLA Ops:
  0.8 0.9 select_reduce_fusion.5
  1.6 1.2 add_divide_fusion.gate
  2.9 0.9 select_reduce_fusion.2
  3.8 0.1 copy.18
  3.9 0.1 reshape.443
  4.0 0.2 convert_reduce_fusion
  4.2 0.6 add_bitcast_fusion.own
  4.8 0.1 add_select_fusion.2
  4.9 23.8 %shard_map.147 = s32[8,8,4,1,128]{4,3,2,1,0:T(1,128)} custom-call(s32[1,128]{1,0:T(1,128)} %add_bitcast_fusion.own), custom_call_target="tpu_custom_call" | custom-call | tf_op jit(solution)/shard_map/pallas_call | solution.py:73
  28.7 0.9 slice_bitcast_fusion.1
  29.7 1.5 fusion.4
  31.1 0.7 select_reduce_fusion.3.fetch
  31.8 0.1 broadcast_in_dim_reshape.4
  31.9 0.7 select_reduce_fusion.4.send
  32.8 0.1 select_reduce_fusion.1
  32.9 0.5 broadcast.643
  33.4 0.7 fusion.45
  34.1 0.1 squeeze.14
  34.2 0.6 fusion.35.found
  34.8 0.2 select_reduce_fusion
  35.0 0.6 reshape.448.heads
  35.6 0.1 copy.19
  35.7 0.7 reshape.446.select
  36.3 0.0 copy-start.1
  36.3 173.6 %shard_map.148 = (bf16[128,2048]{1,0:T(8,128)(2,1)}, bf16[64,128,128]{2,1,0:T(8,128)(2,1)}, bf16[64,128,128]{2,1,0:T(8,128)(2,1)}, f32[16,128]{1,0:T(8,128)}) custom-call(s32[128]{0:T(128)} %reshape.446.select, s32[128]{0:T(128)} %reshape.448.heads, s32[512]{0:T(512)} %fusion.35.found, s32[16]{0:T(128)} %select_reduce_fusion.4.send, ...), custom_call_target="tpu_custom_call" | custom-call | tf_op jit(solution)/shard_map/pallas_call | solution.py:521
  209.9 0.8 reduce_sum.69
  210.8 0.0 copy-done.1
  210.8 0.5 fusion.38
  211.3 1.9 copy.23
  213.2 0.0 copy-start
  213.2 3.3 %copy.24 = bf16[4,16,128,128]{3,2,1,0:T(8,128)(2,1)} copy(bf16[4,16,128,128]{3,2,1,0:T(8,128)(2,1)} %bitcast.19) | data formatting | bytes 4194304
  216.5 0.0 copy-done
  216.5 1.3 copy.25
  (13 shorter events, 0.2 us)
Async XLA Ops:
  36.3 174.4 %copy-start.1 = (f32[16]{0:T(128)S(1)}, f32[16]{0:T(128)}, u32[]{:S(2)}) copy-start(f32[16]{0:T(128)} %param.19) | copy-start | bytes 196
  213.2 3.3 %copy-start = (bf16[64,128,128]{2,1,0:T(8,128)(2,1)S(1)}, bf16[64,128,128]{2,1,0:T(8,128)(2,1)}, u32[]{:S(2)}) copy-start(bf16[64,128,128]{2,1,0:T(8,128)(2,1)} %get-tuple-element.10) | copy-start | bytes 6291460

commit v3 on v2

v3 whole, which is shorter than its diff:
```python
import functools
import math

import jax
import jax.numpy as jnp
from jax import lax
from jax.experimental import pallas as pl
from jax.experimental.pallas import tpu as pltpu
from jax.sharding import PartitionSpec as P

MESH = pl.DeviceIdType.MESH
BF16, F32 = jnp.bfloat16, jnp.float32
NZ, NL, ND = 8, 8, 4
OFFSETS = (3, -4, 2, -3, 1, -2, -1, 0)
NONE = -1e30
CHUNKS = 4
PART = 16 // CHUNKS
UNITS_AFTER, WY_AFTER, WX_AFTER = 1, -1, 2
FIRST = 5


def wrap(value, size):
    return lax.rem(value + 4 * size, size)


def peers(group, layer, lane):
    in_layer = lambda r: (group, layer * NL + wrap(lane + r, NL))
    along_z = lambda r: (group, wrap(layer + r, NZ) * NL + lane)
    in_groups = lambda r: (wrap(group + r, ND), layer * NL + lane)
    return in_layer, along_z, in_groups


def greet(group, layer, lane):
    barrier = pltpu.get_barrier_semaphore()
    in_layer, along_z, in_groups = peers(group, layer, lane)

    @pl.loop(1, 8)
    def _(r):
        pl.semaphore_signal(barrier, inc=1, device_id=in_layer(r), device_id_type=MESH)
        pl.semaphore_signal(barrier, inc=1, device_id=along_z(r), device_id_type=MESH)

    @pl.loop(1, 4)
    def _(r):
        pl.semaphore_signal(barrier, inc=1, device_id=in_groups(r), device_id_type=MESH)

    return lambda: pl.semaphore_wait(barrier, 17)


def remote(src, dst, s, r, to):
    return pltpu.make_async_remote_copy(
        src_ref=src, dst_ref=dst, send_sem=s, recv_sem=r, device_id=to, device_id_type=MESH
    )


def codes(block_home, query_blocks, write_slots):
    place = lax.axis_index("mem")
    lanes = jnp.arange(256, dtype=jnp.int32)
    wanted = query_blocks.reshape(16, 4)
    storage = jnp.sum(
        jnp.where(wanted[:, :, None] == lanes, block_home[:, None, :], 0), axis=-1
    ).reshape(64)
    owner = storage // 4
    count = jnp.arange(64, dtype=jnp.int32)
    rank = jnp.sum(
        ((owner[:, None] == owner[None, :]) & (count[:, None] > count[None, :])).astype(jnp.int32),
        axis=1,
    )
    homes = lax.dynamic_slice_in_dim(block_home, (place % 2) * 8, 8, 0)
    written = jnp.sum(jnp.where(write_slots[:, None] == lanes, homes, 0), axis=-1)
    packed = jnp.concatenate([storage * 2 + rank, written, jnp.zeros((56,), jnp.int32)])
    return packed.reshape(1, 128)


def kernel(
    gate,
    own,
    q_ref,
    kl_ref,
    vl_ref,
    cot_ref,
    mk_ref,
    mv_ref,
    pk_ref,
    pv_ref,
    mixed_ref,
    nk_ref,
    nv_ref,
    part_ref,
    code_all,
    rows,
    ask_v,
    ask,
    put_v,
    put,
    unit_all,
    kv_out,
    kv_in,
    q_all,
    cot_t,
    slot_o,
    slot_s,
    near_o,
    res_o,
    res_s,
    got_o,
    got_s,
    w_out,
    w_mid,
    w_in,
    part,
    g_x,
    g_l,
    g_z,
    c_send,
    c_recv,
    table_sem,
    x_send,
    x_recv,
    kv_send,
    kv_recv,
    q_send,
    q_recv,
    ro_send,
    ro_recv,
    rs_send,
    rs_recv,
    wz_send,
    wz_recv,
    wy_send,
    wy_recv,
    wx_send,
    wx_recv,
    gx_send,
    gx_recv,
    gl_send,
    gl_recv,
    gz_send,
    gz_recv,
):
    group, place = lax.axis_index("dp"), lax.axis_index("mem")
    layer, lane = lax.div(place, NL), lax.rem(place, NL)
    row = lax.div(lane, 2)
    scale = 1.0 / math.sqrt(128.0)

    def at(g, z, l):
        return (g, z * NL + l)

    ready = greet(group, layer, lane)
    in_layer, along_z, in_groups = peers(group, layer, lane)
    code_all[group, lane, layer] = own[...]
    for h in range(16):
        q_all[layer, h] = q_ref[:, h * 128 : (h + 1) * 128]
    for u in range(8):
        unit_all[group, u, 0] = pk_ref[u]
        unit_all[group, u, 1] = pv_ref[u]
    ready()

    def code_copies(step):
        part, to, size = (
            (code_all.at[group, lane, layer], along_z, NZ),
            (code_all.at[group, lane], in_layer, NL),
            (code_all.at[group], in_groups, ND),
        )[step]
        return [
            remote(part, part, c_send.at[step, k], c_recv.at[step, k], to(k))
            for k in range(1, size)
        ]

    def start_all(copies):
        for copy in copies:
            copy.start()

    def wait_all(copies):
        for copy in copies:
            copy.wait()

    start_all(code_copies(0))

    def q_copy(hop, up):
        source = wrap(layer - hop if up else layer + hop, NZ)
        to = at(group, wrap(layer + (1 if up else -1), NZ), lane)
        k = 0 if up else 1
        return remote(
            q_all.at[source], q_all.at[source], q_send.at[k, hop], q_recv.at[k, hop], to
        )

    q_copy(0, True).start()
    q_copy(0, False).start()

    def x_copy(r):
        return remote(
            unit_all.at[group], unit_all.at[group], x_send.at[r], x_recv.at[r], in_groups(r)
        )

    rows_at = lax.broadcasted_iota(jnp.int32, (128, 128), 0)
    cols_at = lax.broadcasted_iota(jnp.int32, (128, 128), 1)
    rows[...] = jnp.zeros_like(rows)
    wait_all(code_copies(0))
    start_all(code_copies(1))
    wait_all(code_copies(1))
    start_all(code_copies(2))

    @pl.loop(1, 4)
    def _(r):
        x_copy(r).start()

    def lay_rows(g):
        @pl.loop(0, NL)
        def _(l):
            for z in range(NZ):
                rows[g, pl.ds(l * NZ + z, 1), :] = code_all[g, l, z]

    def to_scalars(source, target, k):
        copy = pltpu.make_async_copy(source, target, table_sem.at[k])
        copy.start()
        copy.wait()

    def most(allowed, value, none):
        return jnp.max(jnp.where(allowed, value, none), axis=0, keepdims=True)

    lay_rows(group)
    asked = rows[group].T
    real = rows_at < 64
    for k in range(2):
        ask_v[k : k + 1, :] = most(
            real & ((asked >> 3) == place) & ((asked & 1) == k),
            ((asked >> 1) & 3) * 16 + (rows_at >> 2),
            0,
        )
    for k in range(2, 8):
        ask_v[k : k + 1, :] = jnp.zeros((1, 128), jnp.int32)
    mine = rows[group, pl.ds(pl.multiple_of(lane * NZ, NZ), NZ), :]
    ask_v[8:16, :] = jnp.where((mine >> 6) == layer, ((mine >> 3) & 7) * 2 + (mine & 1), -1)
    spots = jnp.where(real & ((asked >> 6) == layer), ((asked >> 3) & 7) * 2 + (asked & 1), -1)
    for k in range(16):
        ask_v[16 + k : 17 + k, :] = most(spots == k, rows_at >> 2, 0)
    to_scalars(ask_v, ask, 0)

    def select(tile, l, k):
        return ask[k, l * NZ + tile]

    def unit_tables():
        wait_all(code_copies(2))
        unit_at, col = rows_at[:8], cols_at[:8]
        to = (col >> 1) * NL + ((row + group + layer) & 3) * 2 + (col & 1)
        come = jnp.full((1, 128), -1, jnp.int32)
        chosen = jnp.zeros((1, 128), jnp.int32)
        for g in range(ND):
            lay_rows(g)
            places = rows[g].T[64:72, :]
            head = ((col >> 3) & 1) * 8 + unit_at
            come = jnp.maximum(
                come, most((col < 64) & ((places >> 2) == place), (places & 3) * 16 + head, -1)
            )
            column = jnp.sum(
                jnp.where(col == lane * NZ + layer, places, 0), axis=1, keepdims=True
            )
            chosen = jnp.maximum(chosen, most((column >> 2) == to, g * 8 + unit_at, 0))
        from_z, from_l = rows_at & 7, rows_at >> 3
        via = (row - (from_l >> 1) - from_z + 16) & 3
        landing = (via * NL + from_l) * 2 + (from_z >> 2)
        came = jnp.broadcast_to(come, (128, 128)).T
        put_v[...] = jnp.zeros_like(put_v)
        put_v[0:1, :] = chosen
        put_v[1:2, :] = most(came == cols_at, landing, -1)
        to_scalars(put_v, put, 1)

    def kv_copy(i, r):
        return remote(
            kv_out.at[i, r],
            kv_in.at[i, lane],
            kv_send.at[i, r],
            kv_recv.at[i, r],
            at(group, layer, wrap(lane + r, NL)),
        )

    def kv_issue(i):
        tile = wrap(layer + OFFSETS[i], NZ)
        for k in range(2):
            code = select(tile, lane, k)
            kv_in[i, lane, 0, k] = mk_ref[code]
            kv_in[i, lane, 1, k] = mv_ref[code]

        @pl.loop(1, 8)
        def _(r):
            for k in range(2):
                code = select(tile, wrap(lane + r, NL), k)
                kv_out[i, r, 0, k] = mk_ref[code]
                kv_out[i, r, 1, k] = mv_ref[code]
            kv_copy(i, r).start()

    for i in range(FIRST):
        kv_issue(i)

    def wz_copy(r, k):
        return remote(
            w_out.at[r, k],
            w_mid.at[k, lax.rem(layer, 4), lax.div(layer, 4)],
            wz_send.at[r, k],
            wz_recv.at[r, k],
            at(group, wrap(layer + r, NZ), lane),
        )

    def send_units():
        @pl.loop(1, 4)
        def _(r):
            x_copy(r).wait_recv()

        for r in range(8):
            to_layer = wrap(layer + r, NZ)
            for k in range(2):
                unit = put[0, to_layer * 2 + k]
                for kv in range(2):
                    slab = unit_all[unit // 8, unit % 8, kv]
                    if r == 0:
                        w_mid[k, lax.rem(layer, 4), lax.div(layer, 4), kv] = slab
                    else:
                        w_out[r, k, kv] = slab
                if r > 0:
                    wz_copy(r, k).start()

    def attend(qh, kh, vt, allowed=None):
        scores = (
            lax.dot_general(kh, qh, (((1,), (1,)), ((), ())), preferred_element_type=F32) * scale
        )
        if allowed is not None:
            scores = jnp.where(allowed, scores, NONE)
        top = jnp.max(scores, axis=0, keepdims=True)
        shifted = jnp.exp(scores - top)
        total = jnp.sum(shifted, axis=0, keepdims=True)
        out = jnp.dot(vt, shifted.astype(BF16), preferred_element_type=F32) * (1.0 / total)
        return out, top + jnp.log(total)

    def near(first):
        for h in range(first, first + 8):
            cols = slice(h * 128, h * 128 + 128)
            near_o[h], _ = attend(
                q_ref[:, cols], kl_ref[:, cols], vl_ref[:, cols].T, rows_at <= cols_at
            )
            cot_t[h] = cot_ref[:, cols].T

    unit_tables()
    for hop in range(4):
        q_copy(hop, True).wait_recv()
        if hop < 3:
            q_copy(hop + 1, True).start()
            q_copy(hop, False).wait_recv()
        if hop < 2:
            q_copy(hop + 1, False).start()
        if hop == UNITS_AFTER:
            send_units()
        if hop in (0, 1):
            near(8 * hop)

    def wy_copy(r):
        peer = wrap(lane + r, NL)
        low = wrap(lax.div(peer, 2) - row - group, 4)
        return remote(
            w_mid.at[lax.rem(peer, 2), low],
            w_in.at[group, lane],
            wy_send.at[r],
            wy_recv.at[r],
            at(group, layer, peer),
        )

    def wx_copy(r):
        return remote(
            w_in.at[group],
            w_in.at[group],
            wx_send.at[r],
            wx_recv.at[r],
            at(wrap(group + r, ND), layer, lane),
        )

    def result_copies(i, c):
        to = at(group, wrap(layer + (1 if OFFSETS[i] > 0 else -1), NZ), lane)
        return (
            remote(res_o.at[i, c], got_o.at[i, c], ro_send.at[i, c], ro_recv.at[i, c], to),
            remote(res_s.at[i, c], got_s.at[i, c], rs_send.at[i, c], rs_recv.at[i, c], to),
        )

    def pass_units():
        @pl.loop(1, 8)
        def _(r):
            for k in range(2):
                wz_copy(r, k).wait_recv()

        low = wrap(-group, 4)
        w_in[group, lane] = w_mid[lax.rem(lane, 2), low]

        @pl.loop(1, 8)
        def _(r):
            wy_copy(r).start()

        for k in range(FIRST, 8):
            kv_issue(k)

    if WY_AFTER < 0:
        pass_units()
    joins = []
    for i, off in enumerate(OFFSETS):
        if off == 0:
            joins.append((OFFSETS.index(1), OFFSETS.index(-1)))
        else:
            further = off + (1 if off > 0 else -1)
            joins.append((OFFSETS.index(further),) if further in OFFSETS else ())

    for i, off in enumerate(OFFSETS):
        tile = wrap(layer + off, NZ)

        @pl.loop(1, 8)
        def _(r):
            kv_copy(i, r).wait_recv()

        @pl.loop(0, 4)
        def _(step):
            for k in range(4):
                s = step * 4 + k
                head = ask[16 + s, lane * NZ + tile]
                kh, vh = kv_in[i, step * 2 + k // 2, 0, k % 2], kv_in[i, step * 2 + k // 2, 1, k % 2]
                out, stat = attend(q_all[tile, head], kh, vh.T)
                slot_o[s] = out
                slot_s[s] = stat

        for c in range(CHUNKS):
            for j in joins[i]:
                for copy in result_copies(j, c):
                    copy.wait_recv()

            @pl.loop(0, PART)
            def _(n):
                h = c * PART + n
                outs, stats = [], []
                for j in range(4):
                    where = ask[8 + tile, h * 4 + j]
                    spot = jnp.maximum(where, 0)
                    outs.append(slot_o[spot])
                    stats.append(jnp.where(where >= 0, slot_s[spot], NONE))
                for j in joins[i]:
                    outs.append(got_o[j, c, n].astype(F32))
                    stats.append(got_s[j, c, pl.ds(n, 1), :])
                top = functools.reduce(jnp.maximum, stats)
                weights = [jnp.exp(stat - top) for stat in stats]
                total = functools.reduce(jnp.add, weights)
                inverse = 1.0 / total
                out = functools.reduce(
                    jnp.add, [(w * inverse) * o for w, o in zip(weights, outs)]
                )
                if off != 0:
                    res_o[i, c, n] = out.astype(BF16)
                    res_s[i, c, pl.ds(n, 1), :] = top + jnp.log(total)
                else:
                    cols = pl.ds(pl.multiple_of(h * 128, 128), 128)
                    opening = gate[h]
                    local = near_o[h]
                    mixed_ref[:, cols] = (opening * out + (1.0 - opening) * local).T.astype(BF16)
                    part[pl.ds(h, 1), :] = jnp.sum(
                        cot_t[h].astype(F32) * (out - local), axis=0, keepdims=True
                    )

            if off != 0:
                for copy in result_copies(i, c):
                    copy.start()

        if i == WY_AFTER:
            pass_units()

        if i == WX_AFTER:
            @pl.loop(1, 8)
            def _(r):
                wy_copy(r).wait_recv()

            @pl.loop(1, 4)
            def _(r):
                wx_copy(r).start()


    def spread(value, held, mine, size, s, r, to):
        held[mine] = value
        copies = [
            remote(held.at[mine], held.at[mine], s.at[k], r.at[k], to(k)) for k in range(1, size)
        ]
        for copy in copies:
            copy.start()
        return copies

    def total_of(held, copies):
        for copy in copies:
            copy.wait()
        return jnp.sum(held[...], axis=0)

    gx = spread(part[...], g_x, group, ND, gx_send, gx_recv, in_groups)

    @pl.loop(1, 4)
    def _(r):
        wx_copy(r).wait_recv()

    gl = spread(total_of(g_x, gx), g_l, lane, NL, gl_send, gl_recv, in_layer)

    @pl.loop(0, 64)
    def _(slab):
        where = put[1, slab]
        spot = jnp.maximum(where, 0)
        for kv, (old, new) in enumerate(((mk_ref, nk_ref), (mv_ref, nv_ref))):
            came = w_in[spot // 16, spot // 2 % 8, spot % 2, kv]
            new[slab] = jnp.where(where >= 0, came, old[slab])

    gz = spread(total_of(g_l, gl), g_z, layer, NZ, gz_send, gz_recv, along_z)

    for hop in range(4):
        q_copy(hop, True).wait_send()
        if hop < 3:
            q_copy(hop, False).wait_send()
    for i, off in enumerate(OFFSETS):
        if off != 0:
            for c in range(CHUNKS):
                for copy in result_copies(i, c):
                    copy.wait_send()

        @pl.loop(1, 8)
        def _(r):
            kv_copy(i, r).wait_send()

    @pl.loop(1, 4)
    def _(r):
        x_copy(r).wait_send()
        wx_copy(r).wait_send()

    @pl.loop(1, 8)
    def _(r):
        wy_copy(r).wait_send()
        for k in range(2):
            wz_copy(r, k).wait_send()

    part_ref[...] = total_of(g_z, gz)


def on_device(
    queries,
    keys_local,
    values_local,
    mem_keys,
    mem_values,
    prev_keys,
    prev_values,
    gate_logit,
    cotangent,
    block_home,
    query_blocks,
    write_slots,
):
    own = codes(block_home, query_blocks, write_slots)
    sigmoid_gate = jax.nn.sigmoid(gate_logit)
    smem, vmem = (pl.BlockSpec(memory_space=space) for space in (pltpu.SMEM, pltpu.VMEM))
    dma = pltpu.SemaphoreType.DMA
    mixed, new_keys, new_values, part = pl.pallas_call(
        kernel,
        out_shape=(
            jax.ShapeDtypeStruct((128, 2048), BF16),
            jax.ShapeDtypeStruct((64, 128, 128), BF16),
            jax.ShapeDtypeStruct((64, 128, 128), BF16),
            jax.ShapeDtypeStruct((16, 128), F32),
        ),
        in_specs=[smem] + [vmem] * 9,
        out_specs=(vmem,) * 4,
        scratch_shapes=[
            pltpu.VMEM((ND, NL, NZ, 1, 128), jnp.int32),
            pltpu.VMEM((ND, 128, 128), jnp.int32),
            pltpu.VMEM((32, 128), jnp.int32),
            pltpu.SMEM((32, 128), jnp.int32),
            pltpu.VMEM((8, 128), jnp.int32),
            pltpu.SMEM((8, 128), jnp.int32),
            pltpu.VMEM((ND, 8, 2, 128, 128), BF16),
            pltpu.VMEM((8, 8, 2, 2, 128, 128), BF16),
            pltpu.VMEM((8, 8, 2, 2, 128, 128), BF16),
            pltpu.VMEM((8, 16, 128, 128), BF16),
            pltpu.VMEM((16, 128, 128), BF16),
            pltpu.VMEM((16, 128, 128), F32),
            pltpu.VMEM((16, 1, 128), F32),
            pltpu.VMEM((16, 128, 128), F32),
            pltpu.VMEM((7, CHUNKS, PART, 128, 128), BF16),
            pltpu.VMEM((7, CHUNKS, PART, 128), F32),
            pltpu.VMEM((7, CHUNKS, PART, 128, 128), BF16),
            pltpu.VMEM((7, CHUNKS, PART, 128), F32),
            pltpu.VMEM((8, 2, 2, 128, 128), BF16),
            pltpu.VMEM((2, 4, 2, 2, 128, 128), BF16),
            pltpu.VMEM((4, 8, 2, 2, 128, 128), BF16),
            pltpu.VMEM((16, 128), F32),
            pltpu.VMEM((ND, 16, 128), F32),
            pltpu.VMEM((NL, 16, 128), F32),
            pltpu.VMEM((NZ, 16, 128), F32),
            dma((3, 8)),
            dma((3, 8)),
            dma((2,)),
            dma((ND,)),
            dma((ND,)),
            dma((8, 8)),
            dma((8, 8)),
            dma((2, 4)),
            dma((2, 4)),
            dma((7, CHUNKS)),
            dma((7, CHUNKS)),
            dma((7, CHUNKS)),
            dma((7, CHUNKS)),
            dma((8, 2)),
            dma((8, 2)),
            dma((8,)),
            dma((8,)),
            dma((4,)),
            dma((4,)),
            dma((ND,)),
            dma((ND,)),
            dma((NL,)),
            dma((NL,)),
            dma((NZ,)),
            dma((NZ,)),
        ],
        compiler_params=pltpu.CompilerParams(
            collective_id=0, has_side_effects=True, vmem_limit_bytes=60 * 1024 * 1024
        ),
    )(
        sigmoid_gate,
        own,
        queries,
        keys_local,
        values_local,
        cotangent,
        mem_keys.reshape(64, 128, 128),
        mem_values.reshape(64, 128, 128),
        prev_keys,
        prev_values,
    )
    total = jnp.sum(part, axis=1)
    gate_grad = sigmoid_gate * (1.0 - sigmoid_gate) * total
    return mixed, new_keys.reshape(mem_keys.shape), new_values.reshape(mem_values.shape), gate_grad


def solution(mesh):
    tokens, slabs = P(("dp", "mem"), None), P("mem", None, None, None)
    units = P(("dp", "mem"), None, None)
    return jax.shard_map(
        on_device,
        mesh=mesh,
        in_specs=(
            tokens,
            tokens,
            tokens,
            slabs,
            slabs,
            units,
            units,
            P(),
            tokens,
            P(),
            units,
            P(("dp", "mem")),
        ),
        out_specs=(tokens, slabs, slabs, P()),
        check_vma=False,
    )
```

time: 218 us -> 183 us (0.84)
  Pallas kernels: 197 us -> 170 us
  other arithmetic: 9.2 us -> 5.11 us
  local copies, waits for them, and re-layouts: 10.4 us -> 6.7 us
    pallas_call x1 -> x0, Pallas kernels: 23.8 us -> none  [gather_codes(): pl.pallas_call(code_kernel, out_shape=jax.ShapeDtypeStruct((NZ, NL, ND, 1...]
    pallas_call x1, Pallas kernels: 174 us -> 170 us  [on_device(): pl.pallas_call(kernel, out_shape=(jax.ShapeDtypeStruct((128, 2048), BF16)...]
where the time goes in v3:
time: 183 us
  Pallas kernels  170 us (93%)
  local copies, waits for them, and re-layouts  6.7 us (4%)
  other arithmetic  5.11 us (3%)
    pallas_call x1, Pallas kernels, on_device(): pl.pallas_call(kernel, out_shape=(jax.ShapeDtypeStruct((128, 2048), BF16)...  170 us
    unnamed x7, local copies, waits for them, and re-layouts  6.51 us

profile of v3, /device:TPU:1, one launch (start us, length us, event | category | flops | bytes accessed | tf_op | source)
XLA Modules:
  0.0 182.9 jit_solution(6697197368803550668)
XLA Ops:
  0.6 0.9 select_reduce_fusion.1
  1.5 1.2 add_divide_fusion.gate
  2.7 0.9 select_reduce_fusion
  3.6 0.1 copy.18
  3.7 0.1 reshape.85
  3.8 0.2 convert_reduce_fusion
  4.0 0.6 add_bitcast_fusion.own
  4.6 0.0 copy-start.1
  4.6 170.4 %shard_map.147 = (bf16[128,2048]{1,0:T(8,128)(2,1)}, bf16[64,128,128]{2,1,0:T(8,128)(2,1)}, bf16[64,128,128]{2,1,0:T(8,128)(2,1)}, f32[16,128]{1,0:T(8,128)}) custom-call(f32[16]{0:T(128)} %add_divide_fusion.gate, s32[1,128]{1,0:T(1,128)} %add_bitcast_fusion.own, bf16[128,2048]{1,0:T(8,128)(2,1)} %q_ref.1, bf16[128,2048]{1,0:T(8,128)(2,1)} %kl_ref.1, ...), custom_call_target="tpu_custom_call" | custom-call | tf_op jit(solution)/shard_map/pallas_call | solution.py:556
  175.0 0.8 reduce_sum.39
  175.8 0.0 copy-done.1
  175.8 0.5 fusion.1
  176.4 1.9 %copy.22 = bf16[128,2048]{1,0:T(8,128)(2,1)} copy(bf16[128,2048]{1,0:T(8,128)(2,1)} %get-tuple-element.16) | data formatting | bytes 1048576
  178.2 0.0 copy-start
  178.2 3.3 %copy.23 = bf16[4,16,128,128]{3,2,1,0:T(8,128)(2,1)} copy(bf16[4,16,128,128]{3,2,1,0:T(8,128)(2,1)} %bitcast.10) | data formatting | bytes 4194304
  181.6 0.0 copy-done
  181.6 1.3 copy.24
  (3 shorter events, 0.0 us)
Async XLA Ops:
  4.6 171.2 %copy-start.1 = (f32[16]{0:T(128)S(1)}, f32[16]{0:T(128)}, u32[]{:S(2)}) copy-start(f32[16]{0:T(128)} %param.19) | copy-start | bytes 196
  178.2 3.3 %copy-start = (bf16[64,128,128]{2,1,0:T(8,128)(2,1)S(1)}, bf16[64,128,128]{2,1,0:T(8,128)(2,1)}, u32[]{:S(2)}) copy-start(bf16[64,128,128]{2,1,0:T(8,128)(2,1)} %get-tuple-element.10) | copy-start | bytes 6291460

commit v4 on v3

--- a/solution.py
+++ b/solution.py
@@ -11,7 +11,7 @@
 MESH = pl.DeviceIdType.MESH
 BF16, F32 = jnp.bfloat16, jnp.float32
 NZ, NL, ND = 8, 8, 4
-OFFSETS = (3, -4, 2, -3, 1, -2, -1, 0)
+OFFSETS = (-4, 3, -3, 2, -2, 1, -1, 0)
 NONE = -1e30
 CHUNKS = 4
 PART = 16 // CHUNKS
@@ -75,17 +75,22 @@
     gate,
     own,
     q_ref,
-    kl_ref,
-    vl_ref,
-    cot_ref,
-    mk_ref,
-    mv_ref,
+    kl_hbm,
+    vl_hbm,
+    cot_hbm,
+    mk_hbm,
+    mv_hbm,
     pk_ref,
     pv_ref,
     mixed_ref,
     nk_ref,
     nv_ref,
     part_ref,
+    kl_ref,
+    vl_ref,
+    cot_ref,
+    mk_ref,
+    mv_ref,
     code_all,
     rows,
     ask_v,
@@ -111,6 +116,7 @@
     g_x,
     g_l,
     g_z,
+    load_sem,
     c_send,
     c_recv,
     table_sem,
@@ -147,6 +153,20 @@
 
     ready = greet(group, layer, lane)
     in_layer, along_z, in_groups = peers(group, layer, lane)
+    loads = [
+        pltpu.make_async_copy(source, target, load_sem.at[k])
+        for k, (source, target) in enumerate(
+            (
+                (mk_hbm, mk_ref),
+                (mv_hbm, mv_ref),
+                (kl_hbm, kl_ref),
+                (vl_hbm, vl_ref),
+                (cot_hbm, cot_ref),
+            )
+        )
+    ]
+    for load in loads:
+        load.start()
     code_all[group, lane, layer] = own[...]
     for h in range(16):
         q_all[layer, h] = q_ref[:, h * 128 : (h + 1) * 128]
@@ -180,9 +200,8 @@
         source = wrap(layer - hop if up else layer + hop, NZ)
         to = at(group, wrap(layer + (1 if up else -1), NZ), lane)
         k = 0 if up else 1
-        return remote(
-            q_all.at[source], q_all.at[source], q_send.at[k, hop], q_recv.at[k, hop], to
-        )
+        part = q_all.at[source, pl.ds(8 * k, 8)] if hop == 3 else q_all.at[source]
+        return remote(part, part, q_send.at[k, hop], q_recv.at[k, hop], to)
 
     q_copy(0, True).start()
     q_copy(0, False).start()
@@ -289,6 +308,8 @@
                 kv_out[i, r, 1, k] = mv_ref[code]
             kv_copy(i, r).start()
 
+    for load in loads:
+        load.wait()
     for i in range(FIRST):
         kv_issue(i)
 
@@ -344,8 +365,8 @@
         q_copy(hop, True).wait_recv()
         if hop < 3:
             q_copy(hop + 1, True).start()
-            q_copy(hop, False).wait_recv()
-        if hop < 2:
+        q_copy(hop, False).wait_recv()
+        if hop < 3:
             q_copy(hop + 1, False).start()
         if hop == UNITS_AFTER:
             send_units()
@@ -373,7 +394,8 @@
         )
 
     def result_copies(i, c):
-        to = at(group, wrap(layer + (1 if OFFSETS[i] > 0 else -1), NZ), lane)
+        up = OFFSETS[i] > 0 or (OFFSETS[i] == -4 and c >= CHUNKS // 2)
+        to = at(group, wrap(layer + (1 if up else -1), NZ), lane)
         return (
             remote(res_o.at[i, c], got_o.at[i, c], ro_send.at[i, c], ro_recv.at[i, c], to),
             remote(res_s.at[i, c], got_s.at[i, c], rs_send.at[i, c], rs_recv.at[i, c], to),
@@ -397,13 +419,13 @@
 
     if WY_AFTER < 0:
         pass_units()
-    joins = []
-    for i, off in enumerate(OFFSETS):
+    def joins(i, c):
+        off = OFFSETS[i]
         if off == 0:
-            joins.append((OFFSETS.index(1), OFFSETS.index(-1)))
-        else:
-            further = off + (1 if off > 0 else -1)
-            joins.append((OFFSETS.index(further),) if further in OFFSETS else ())
+            return OFFSETS.index(1), OFFSETS.index(-1)
+        if abs(off) == 3:
+            return (0,) if (off > 0) == (c >= CHUNKS // 2) else ()
+        return () if off == -4 else (OFFSETS.index(off + (1 if off > 0 else -1)),)
 
     for i, off in enumerate(OFFSETS):
         tile = wrap(layer + off, NZ)
@@ -423,7 +445,7 @@
                 slot_s[s] = stat
 
         for c in range(CHUNKS):
-            for j in joins[i]:
+            for j in joins(i, c):
                 for copy in result_copies(j, c):
                     copy.wait_recv()
 
@@ -436,7 +458,7 @@
                     spot = jnp.maximum(where, 0)
                     outs.append(slot_o[spot])
                     stats.append(jnp.where(where >= 0, slot_s[spot], NONE))
-                for j in joins[i]:
+                for j in joins(i, c):
                     outs.append(got_o[j, c, n].astype(F32))
                     stats.append(got_s[j, c, pl.ds(n, 1), :])
                 top = functools.reduce(jnp.maximum, stats)
@@ -509,8 +531,7 @@
 
     for hop in range(4):
         q_copy(hop, True).wait_send()
-        if hop < 3:
-            q_copy(hop, False).wait_send()
+        q_copy(hop, False).wait_send()
     for i, off in enumerate(OFFSETS):
         if off != 0:
             for c in range(CHUNKS):
@@ -551,7 +572,9 @@
 ):
     own = codes(block_home, query_blocks, write_slots)
     sigmoid_gate = jax.nn.sigmoid(gate_logit)
-    smem, vmem = (pl.BlockSpec(memory_space=space) for space in (pltpu.SMEM, pltpu.VMEM))
+    smem, vmem, later = (
+        pl.BlockSpec(memory_space=space) for space in (pltpu.SMEM, pltpu.VMEM, pl.ANY)
+    )
     dma = pltpu.SemaphoreType.DMA
     mixed, new_keys, new_values, part = pl.pallas_call(
         kernel,
@@ -561,9 +584,14 @@
             jax.ShapeDtypeStruct((64, 128, 128), BF16),
             jax.ShapeDtypeStruct((16, 128), F32),
         ),
-        in_specs=[smem] + [vmem] * 9,
+        in_specs=[smem] + [vmem] * 2 + [later] * 5 + [vmem] * 2,
         out_specs=(vmem,) * 4,
         scratch_shapes=[
+            pltpu.VMEM((128, 2048), BF16),
+            pltpu.VMEM((128, 2048), BF16),
+            pltpu.VMEM((128, 2048), BF16),
+            pltpu.VMEM((64, 128, 128), BF16),
+            pltpu.VMEM((64, 128, 128), BF16),
             pltpu.VMEM((ND, NL, NZ, 1, 128), jnp.int32),
             pltpu.VMEM((ND, 128, 128), jnp.int32),
             pltpu.VMEM((32, 128), jnp.int32),
@@ -589,6 +617,7 @@
             pltpu.VMEM((ND, 16, 128), F32),
             pltpu.VMEM((NL, 16, 128), F32),
             pltpu.VMEM((NZ, 16, 128), F32),
+            dma((5,)),
             dma((3, 8)),
             dma((3, 8)),
             dma((2,)),

time: 183 us -> 176 us (0.962)
  Pallas kernels: 170 us -> 163 us
    pallas_call x1, Pallas kernels: 170 us -> 163 us  [on_device(): pl.pallas_call(kernel, out_shape=(jax.ShapeDtypeStruct((128, 2048), BF16)...]
where the time goes in v4:
time: 176 us
  Pallas kernels  163 us (93%)
  local copies, waits for them, and re-layouts  6.7 us (4%)
  other arithmetic  5.11 us (3%)
    pallas_call x1, Pallas kernels, on_device(): pl.pallas_call(kernel, out_shape=(jax.ShapeDtypeStruct((128, 2048), BF16)...  163 us
    unnamed x7, local copies, waits for them, and re-layouts  6.51 us

profile of v4, /device:TPU:1, one launch (start us, length us, event | category | flops | bytes accessed | tf_op | source)
XLA Modules:
  0.0 175.5 jit_solution(1168819732725393695)
XLA Ops:
  0.6 0.9 select_reduce_fusion.1
  1.5 1.2 add_divide_fusion.gate
  2.7 0.9 select_reduce_fusion
  3.6 0.1 copy.18
  3.7 0.1 reshape.85
  3.8 0.2 convert_reduce_fusion
  4.0 0.6 add_bitcast_fusion.own
  4.6 0.0 copy-start.1
  4.6 163.0 %shard_map.147 = (bf16[128,2048]{1,0:T(8,128)(2,1)}, bf16[64,128,128]{2,1,0:T(8,128)(2,1)}, bf16[64,128,128]{2,1,0:T(8,128)(2,1)}, f32[16,128]{1,0:T(8,128)}) custom-call(f32[16]{0:T(128)} %add_divide_fusion.gate, s32[1,128]{1,0:T(1,128)} %add_bitcast_fusion.own, bf16[128,2048]{1,0:T(8,128)(2,1)} %q_ref.1, bf16[128,2048]{1,0:T(8,128)(2,1)} %kl_hbm.1, ...), custom_call_target="tpu_custom_call" | custom-call | tf_op jit(solution)/shard_map/pallas_call | solution.py:579
  167.7 0.8 reduce_sum.39
  168.5 0.0 copy-done.1
  168.5 0.5 fusion.1
  169.0 1.9 %copy.22 = bf16[128,2048]{1,0:T(8,128)(2,1)} copy(bf16[128,2048]{1,0:T(8,128)(2,1)} %get-tuple-element.16) | data formatting | bytes 1048576
  170.9 0.0 copy-start
  170.9 3.3 %copy.23 = bf16[4,16,128,128]{3,2,1,0:T(8,128)(2,1)} copy(bf16[4,16,128,128]{3,2,1,0:T(8,128)(2,1)} %bitcast.10) | data formatting | bytes 4194304
  174.2 0.0 copy-done
  174.2 1.3 copy.24
  (3 shorter events, 0.0 us)
Async XLA Ops:
  4.6 163.9 %copy-start.1 = (f32[16]{0:T(128)S(1)}, f32[16]{0:T(128)}, u32[]{:S(2)}) copy-start(f32[16]{0:T(128)} %param.19) | copy-start | bytes 196
  170.9 3.3 %copy-start = (bf16[64,128,128]{2,1,0:T(8,128)(2,1)S(1)}, bf16[64,128,128]{2,1,0:T(8,128)(2,1)}, u32[]{:S(2)}) copy-start(bf16[64,128,128]{2,1,0:T(8,128)(2,1)} %get-tuple-element.10) | copy-start | bytes 6291460

commit v5 on v4

--- a/solution.py
+++ b/solution.py
@@ -194,7 +194,16 @@
         for copy in copies:
             copy.wait()
 
+    def x_copy(r):
+        return remote(
+            unit_all.at[group], unit_all.at[group], x_send.at[r], x_recv.at[r], in_groups(r)
+        )
+
     start_all(code_copies(0))
+
+    @pl.loop(1, 4)
+    def _(r):
+        x_copy(r).start()
 
     def q_copy(hop, up):
         source = wrap(layer - hop if up else layer + hop, NZ)
@@ -205,11 +214,6 @@
 
     q_copy(0, True).start()
     q_copy(0, False).start()
-
-    def x_copy(r):
-        return remote(
-            unit_all.at[group], unit_all.at[group], x_send.at[r], x_recv.at[r], in_groups(r)
-        )
 
     rows_at = lax.broadcasted_iota(jnp.int32, (128, 128), 0)
     cols_at = lax.broadcasted_iota(jnp.int32, (128, 128), 1)
@@ -218,10 +222,6 @@
     start_all(code_copies(1))
     wait_all(code_copies(1))
     start_all(code_copies(2))
-
-    @pl.loop(1, 4)
-    def _(r):
-        x_copy(r).start()
 
     def lay_rows(g):
         @pl.loop(0, NL)
@@ -360,7 +360,6 @@
             )
             cot_t[h] = cot_ref[:, cols].T
 
-    unit_tables()
     for hop in range(4):
         q_copy(hop, True).wait_recv()
         if hop < 3:
@@ -369,6 +368,7 @@
         if hop < 3:
             q_copy(hop + 1, False).start()
         if hop == UNITS_AFTER:
+            unit_tables()
             send_units()
         if hop in (0, 1):
             near(8 * hop)

time: 176 us -> 168 us (0.955)
  Pallas kernels: 163 us -> 155 us
    pallas_call x1, Pallas kernels: 163 us -> 155 us  [on_device(): pl.pallas_call(kernel, out_shape=(jax.ShapeDtypeStruct((128, 2048), BF16)...]
where the time goes in v5:
time: 168 us; the launch traced here: 167 us
  Pallas kernels  155 us (92%)
  local copies, waits for them, and re-layouts  6.7 us (4%)
  other arithmetic  5.11 us (3%)
    pallas_call x1, Pallas kernels, on_device(): pl.pallas_call(kernel, out_shape=(jax.ShapeDtypeStruct((128, 2048), BF16)...  155 us
    unnamed x7, local copies, waits for them, and re-layouts  6.51 us

profile of v5, /device:TPU:1, one launch (start us, length us, event | category | flops | bytes accessed | tf_op | source)
XLA Modules:
  0.0 167.5 jit_solution(2323859868302378847)
XLA Ops:
  0.6 0.9 select_reduce_fusion.1
  1.5 1.2 add_divide_fusion.gate
  2.7 0.9 select_reduce_fusion
  3.6 0.1 copy.18
  3.7 0.1 reshape.85
  3.8 0.2 convert_reduce_fusion
  4.0 0.6 add_bitcast_fusion.own
  4.6 0.0 copy-start.1
  4.6 155.0 %shard_map.147 = (bf16[128,2048]{1,0:T(8,128)(2,1)}, bf16[64,128,128]{2,1,0:T(8,128)(2,1)}, bf16[64,128,128]{2,1,0:T(8,128)(2,1)}, f32[16,128]{1,0:T(8,128)}) custom-call(f32[16]{0:T(128)} %add_divide_fusion.gate, s32[1,128]{1,0:T(1,128)} %add_bitcast_fusion.own, bf16[128,2048]{1,0:T(8,128)(2,1)} %q_ref.1, bf16[128,2048]{1,0:T(8,128)(2,1)} %kl_hbm.1, ...), custom_call_target="tpu_custom_call" | custom-call | tf_op jit(solution)/shard_map/pallas_call | solution.py:579
  159.6 0.8 reduce_sum.39
  160.4 0.0 copy-done.1
  160.4 0.5 fusion.1
  161.0 1.9 %copy.22 = bf16[128,2048]{1,0:T(8,128)(2,1)} copy(bf16[128,2048]{1,0:T(8,128)(2,1)} %get-tuple-element.16) | data formatting | bytes 1048576
  162.8 0.0 copy-start
  162.8 3.3 %copy.23 = bf16[4,16,128,128]{3,2,1,0:T(8,128)(2,1)} copy(bf16[4,16,128,128]{3,2,1,0:T(8,128)(2,1)} %bitcast.10) | data formatting | bytes 4194304
  166.1 0.0 copy-done
  166.1 1.3 copy.24
  (3 shorter events, 0.0 us)
Async XLA Ops:
  4.6 155.8 %copy-start.1 = (f32[16]{0:T(128)S(1)}, f32[16]{0:T(128)}, u32[]{:S(2)}) copy-start(f32[16]{0:T(128)} %param.19) | copy-start | bytes 196
  162.8 3.3 %copy-start = (bf16[64,128,128]{2,1,0:T(8,128)(2,1)S(1)}, bf16[64,128,128]{2,1,0:T(8,128)(2,1)}, u32[]{:S(2)}) copy-start(bf16[64,128,128]{2,1,0:T(8,128)(2,1)} %get-tuple-element.10) | copy-start | bytes 6291460
